TPU v7x, 256 devices: a whole 4x4x8 slice. The times are simulated.
256 devices in a mesh: cls: 32 (over x, z), img: 8 (over y, core).
Axes of the slice: x: 4, y: 4, z: 8, core: 2. Of those that a mesh axis runs over, the one named last changes fastest.
Arguments:
- images: bfloat16 [4096, 9216], P(('cls', 'img')), may hold values from -9 to 9
- ctf: bfloat16 [4096, 4608], P(('cls', 'img')), may hold values from -1 to 1
- classes: int32 [4096, 4], P(('cls', 'img')), may hold values from 0 to 223, as said below
- class_place: int32 [224], replicated, may hold values from 0 to 223, as said below
- references: bfloat16 [224, 9216], P('cls'), may hold values from -3 to 3
- sigma2: float32 [64], replicated, may hold values from 0.05 to 4, as said below
Outputs:
- new_references: float32 [224, 9216], P('cls', 'img')
Inputs may be any that keep to these rules, and one draw needn't show every extreme that they name: Each particle names 4 different classes whose table rows class_place[k] lie in 4 different groups of 7 consecutive table rows. Among the 16 particles of one device (aligned blocks of 16 rows) at most 8 list entries fall in one group, and in every block some group receives exactly 8. A permutation: class k is held in table row class_place[k]. `sigma2`: positive noise powers.
All inputs are finite; a program needn't handle non-finite values.
Results may differ from a plain program's by a relative error of at most 0.0018.
Values may be sent and summed in bfloat16 or wider, within the bound.
No kernel may reach another device: no remote copies, remote signals or barrier semaphores. Data moves between devices by JAX's collectives and lax.ppermute only.
A program may use at most 128 MiB of HBM per device.

v0:
```python
import math

import jax
import jax.numpy as jnp
from jax import lax
from jax.sharding import PartitionSpec as P

CAP = 8


NEGATIVE = -1e30


def sent_together(arrays, axis, split_dim, concat_dim, along):
    widths = [a.shape[along] for a in arrays]
    both = jnp.concatenate(arrays, axis=along)
    out = lax.all_to_all(both, axis, split_axis=split_dim, concat_axis=concat_dim, tiled=True)
    return tuple(jnp.split(out, [sum(widths[:k]) for k in range(1, len(widths))], axis=along))


def from_everyone(x, axis):
    peers = lax.axis_size(axis)
    return lax.all_to_all(jnp.broadcast_to(x[None], (peers, *x.shape)), axis, 0, 0, tiled=True)


def joined_by_halves(pieces, combine):
    while len(jax.tree.leaves(pieces)[0]) > 1:
        pieces = jax.vmap(combine)(
            *(jax.tree.map(lambda part: part[side::2], pieces) for side in (0, 1))
        )
    return jax.tree.map(lambda part: part[0], pieces)


def joined_all(x, axis, combine):
    pieces = jax.tree.map(lambda part: from_everyone(part, axis), x)
    return joined_by_halves(pieces, combine)


def in_blocks(x, dim, peers):
    before, after = (x.shape[:dim], x.shape[dim + 1 :])
    return jnp.moveaxis(x.reshape(*before, peers, -1, *after), dim, 0)


def sent_and_summed(x, axis, dim):
    pieces = in_blocks(x, dim, lax.axis_size(axis))
    arrived = lax.all_to_all(pieces, axis, split_axis=0, concat_axis=0, tiled=True)
    return arrived.sum(axis=0)


def combine_stats(earlier, later):
    highest = jnp.maximum(earlier[0], later[0])
    summed = earlier[1] * jnp.exp(earlier[0] - highest) + later[1] * jnp.exp(later[0] - highest)
    return (highest, summed)


def wave_tables(angles):
    index = jnp.arange(angles, dtype=jnp.int32)
    phase = index[:, None] * index[None, :] % angles
    radians = phase.astype(jnp.float32) * (2.0 * math.pi / angles)
    return (jnp.cos(radians), jnp.sin(radians))


def forward_wave(values, cos_table, sin_table):
    real_part = jnp.matmul(values, cos_table, precision=lax.Precision.HIGHEST)
    imag_part = -jnp.matmul(values, sin_table, precision=lax.Precision.HIGHEST)
    return (real_part, imag_part)


def inverse_wave(real_part, imag_part, cos_table, sin_table):
    angles = cos_table.shape[0]
    summed = jnp.matmul(real_part, cos_table, precision=lax.Precision.HIGHEST) - jnp.matmul(
        imag_part, sin_table, precision=lax.Precision.HIGHEST
    )
    return summed / angles


def on_device(images, ctf, classes, class_place, references, sigma2):
    shells = sigma2.shape[0]
    angles = ctf.shape[1] // shells
    particles = images.shape[0]
    per_owner = references.shape[0]
    owners = lax.axis_size("cls")
    my_owner = lax.axis_index("cls")
    scaling = (
        ctf.astype(jnp.float32).reshape(particles, shells, angles) * (1.0 / sigma2)[None, :, None]
    )
    weighted = (
        (images.astype(jnp.float32).reshape(particles, shells, 2, angles) * scaling[:, :, None, :])
        .astype(jnp.bfloat16)
        .reshape(particles, -1)
    )
    ctf_power = (
        (ctf.astype(jnp.float32).reshape(particles, shells, angles) * scaling)
        .astype(jnp.bfloat16)
        .reshape(particles, -1)
    )
    lookup = classes[:, :, None] == jnp.arange(class_place.shape[0], dtype=jnp.int32)[None, None, :]
    table_rows = jnp.sum(jnp.where(lookup, class_place[None, None, :], 0), axis=2)
    group_size = owners * particles
    owner_of = (table_rows // per_owner).reshape(-1)
    hits = owner_of[:, None] == jnp.arange(owners, dtype=jnp.int32)[None, :]
    before = jnp.cumsum(hits.astype(jnp.int32), axis=0) - 1
    position = jnp.sum(jnp.where(hits, before, 0), axis=1)
    slot_of = owner_of * CAP + position
    slot_count = owners * CAP
    chosen = slot_of[None, :] == jnp.arange(slot_count, dtype=jnp.int32)[:, None]
    filled = jnp.any(chosen, axis=1)
    pick_index = jnp.sum(
        jnp.where(chosen, jnp.arange(slot_of.shape[0], dtype=jnp.int32)[None, :], 0), axis=1
    )
    source_row = pick_index // classes.shape[1]
    send_weighted = jnp.where(filled[:, None], weighted[source_row], 0)
    send_power = jnp.where(filled[:, None], ctf_power[source_row], 0)
    send_class = jnp.where(filled, table_rows.reshape(-1)[pick_index] % per_owner, -1)
    send_particle = my_owner * particles + source_row
    received = (
        *sent_together(
            (send_weighted.reshape(owners, CAP, -1), send_power.reshape(owners, CAP, -1)),
            "cls",
            0,
            0,
            2,
        ),
        *sent_together(
            (send_class.reshape(owners, CAP), send_particle.reshape(owners, CAP)), "cls", 0, 0, 1
        ),
    )
    row_weighted = received[0].reshape(slot_count, -1)
    row_power = received[1].reshape(slot_count, -1)
    row_class = received[2].reshape(slot_count)
    row_particle = received[3].reshape(slot_count)
    row_count = row_weighted.shape[0]
    block_size = 128
    block_count = row_count // block_size
    cos_table, sin_table = wave_tables(angles)
    ref_table = references.astype(jnp.float32).reshape(per_owner, shells, 2, angles)
    table_power = jnp.sum(ref_table * ref_table, axis=2).astype(jnp.bfloat16).astype(jnp.float32)
    ref_real, ref_imag = forward_wave(ref_table, cos_table, sin_table)
    power_real, power_imag = forward_wave(table_power, cos_table, sin_table)
    block_weighted = row_weighted.reshape(block_count, block_size, shells, 2, angles)
    block_power = row_power.reshape(block_count, block_size, shells, angles)
    block_class = row_class.reshape(block_count, block_size)

    def score_block(block_data):
        weight_rows, power_rows, class_rows = block_data
        safe_class = jnp.clip(class_rows, 0, per_owner - 1)
        weight_real, weight_imag = forward_wave(
            weight_rows.astype(jnp.float32), cos_table, sin_table
        )
        ctf_real, ctf_imag = forward_wave(power_rows.astype(jnp.float32), cos_table, sin_table)
        match_real = ref_real[safe_class]
        match_imag = ref_imag[safe_class]
        cross_real = jnp.sum(weight_real * match_real + weight_imag * match_imag, axis=(1, 2))
        cross_imag = jnp.sum(weight_imag * match_real - weight_real * match_imag, axis=(1, 2))
        spot_real = power_real[safe_class]
        spot_imag = power_imag[safe_class]
        quad_real = jnp.sum(ctf_real * spot_real + ctf_imag * spot_imag, axis=1)
        quad_imag = jnp.sum(ctf_imag * spot_real - ctf_real * spot_imag, axis=1)
        return inverse_wave(
            cross_real - 0.5 * quad_real, cross_imag - 0.5 * quad_imag, cos_table, sin_table
        )

    logits = lax.map(score_block, (block_weighted, block_power, block_class)).reshape(
        row_count, angles
    )
    usable = row_class >= 0
    local_max = jnp.max(logits, axis=1)
    local_sum = jnp.sum(jnp.exp(logits - local_max[:, None]), axis=1)
    member = (row_particle[:, None] == jnp.arange(group_size, dtype=jnp.int32)[None, :]) & usable[
        :, None
    ]
    part_max = jnp.max(jnp.where(member, local_max[:, None], NEGATIVE), axis=0)
    part_sum = jnp.sum(jnp.where(member, local_sum[:, None], 0.0), axis=0)
    whole_max, whole_sum = joined_all((part_max, part_sum), "cls", combine_stats)
    row_max = whole_max[row_particle]
    row_sum = whole_sum[row_particle]
    posterior = jnp.where(
        usable[:, None], jnp.exp(logits - row_max[:, None]) / row_sum[:, None], 0.0
    ).astype(jnp.bfloat16)
    block_posterior = posterior.reshape(block_count, block_size, angles)

    def gather_block(totals, block_data):
        num_real, num_imag, den_real, den_imag = totals
        weight_rows, power_rows, class_rows, post_rows = block_data
        weight_real, weight_imag = forward_wave(
            weight_rows.astype(jnp.float32), cos_table, sin_table
        )
        ctf_real, ctf_imag = forward_wave(power_rows.astype(jnp.float32), cos_table, sin_table)
        post_real, post_imag = forward_wave(post_rows.astype(jnp.float32), cos_table, sin_table)
        owned = (class_rows[:, None] == jnp.arange(per_owner, dtype=jnp.int32)[None, :]).astype(
            jnp.float32
        )
        pr_four = post_real[:, None, None, :]
        pi_four = post_imag[:, None, None, :]
        pr_three = post_real[:, None, :]
        pi_three = post_imag[:, None, :]
        num_real = num_real + jnp.einsum(
            "bk,bsqf->ksqf",
            owned,
            weight_real * pr_four + weight_imag * pi_four,
            precision=lax.Precision.HIGHEST,
        )
        num_imag = num_imag + jnp.einsum(
            "bk,bsqf->ksqf",
            owned,
            weight_imag * pr_four - weight_real * pi_four,
            precision=lax.Precision.HIGHEST,
        )
        den_real = den_real + jnp.einsum(
            "bk,bsf->ksf",
            owned,
            ctf_real * pr_three + ctf_imag * pi_three,
            precision=lax.Precision.HIGHEST,
        )
        den_imag = den_imag + jnp.einsum(
            "bk,bsf->ksf",
            owned,
            ctf_imag * pr_three - ctf_real * pi_three,
            precision=lax.Precision.HIGHEST,
        )
        return ((num_real, num_imag, den_real, den_imag), None)

    num_zero = jnp.zeros((per_owner, shells, 2, angles), jnp.float32)
    den_zero = jnp.zeros((per_owner, shells, angles), jnp.float32)
    sums_hat, unused = lax.scan(
        gather_block,
        (num_zero, num_zero, den_zero, den_zero),
        (block_weighted, block_power, block_class, block_posterior),
    )
    numerator = inverse_wave(sums_hat[0], sums_hat[1], cos_table, sin_table).reshape(per_owner, -1)
    denominator = inverse_wave(sums_hat[2], sums_hat[3], cos_table, sin_table).reshape(
        per_owner, -1
    )
    num_share, den_share = (
        sent_and_summed(numerator, "img", 1),
        sent_and_summed(denominator, "img", 1),
    )
    updated = num_share.reshape(per_owner, -1, 2, angles) / (
        den_share.reshape(per_owner, -1, 1, angles) + 1.0
    )
    return updated.reshape(per_owner, -1)


def solution(mesh):
    in_specs = (
        P(("cls", "img"), None),
        P(("cls", "img"), None),
        P(("cls", "img"), None),
        P(),
        P("cls", None),
        P(),
    )
    out_specs = P("cls", "img")
    return jax.shard_map(
        on_device, mesh=mesh, in_specs=in_specs, out_specs=out_specs, check_vma=False
    )
```

profile of v0, /device:TPU:32, one launch (start us, length us, event | category | flops | bytes accessed | tf_op | source)
XLA Modules:
  0.0 542.6 jit_solution(13410750705118385550)
XLA Ops:
  4.7 11.2 %all-to-all-start = ((s32[32,1,16]{2,1,0:T(1,128)}), s32[32,1,16]{2,1,0:T(1,128)S(1)}, u32[]{:S(2)}, u32[]{:S(2)}) async-start(s32[32,1,16]{2,1,0:T(1,128)} %bitcast.3), calls=%async_computation | async-start | bytes 32768 | tf_op jit(solution)/shard_map/all_to_all | solution.py:17
  20.1 5.7 %gather_fusion.5 = bf16[256,9216]{1,0:T(8,128)(2,1)} fusion(bf16[16,9216]{1,0:T(8,128)(2,1)S(1)} %multiply_convert_fusion, s32[1024]{0:T(1024)S(1)} %pad_clamp_fusion.2), kind=kCustom, calls=%fused_computation.5 | custom fusion | bytes 9438208 | tf_op jit(solution)/shard_map/gather | solution.py:112
  25.7 4.9 bitcast_select_fusion
  37.7 5.0 pad_maximum_fusion
  42.8 10.3 %all-to-all-start.1 = ((bf16[32,8,13824]{2,1,0:T(8,128)(2,1)}), bf16[32,8,13824]{2,1,0:T(8,128)(2,1)}, u32[]{:S(2)}, u32[]{:S(2)}) async-start(bf16[32,8,13824]{2,1,0:T(8,128)(2,1)} %pad_maximum_fusion), calls=%async_computation.1 | async-start | bytes 14155776 | tf_op jit(solution)/shard_map/all_to_all | solution.py:17
  59.2 149.8 %all-to-all-done.1 = bf16[32,8,13824]{2,1,0:T(8,128)(2,1)} async-done(((bf16[32,8,13824]{2,1,0:T(8,128)(2,1)}), bf16[32,8,13824]{2,1,0:T(8,128)(2,1)}, u32[]{:S(2)}, u32[]{:S(2)}) %all-to-all-start.1) | async-done | bytes 7077920 | tf_op jit(solution)/shard_map/all_to_all | solution.py:17
  213.8 35.0 %reshape_reshape.16 = bf16[2,128,64,2,72]{4,3,2,1,0:T(2,128)(2,1)} reshape(bf16[32,8,9216]{2,1,0:T(8,128)(2,1)} %split.17) | data formatting | bytes 9437184 | tf_op jit(solution)/shard_map/reshape;reshape | solution.py:140
  248.7 17.8 %copy.106 = bf16[2,128,64,2,72]{1,4,3,2,0:T(8,128)(2,1)} copy(bf16[2,128,64,2,72]{4,3,2,1,0:T(2,128)(2,1)} %reshape_reshape.16) | data formatting | bytes 9437184
  269.8 11.2 %reshape_reshape.17 = bf16[2,128,64,72]{3,2,1,0:T(8,128)(2,1)} reshape(bf16[32,8,4608]{2,1,0:T(8,128)(2,1)} %split.18) | data formatting | bytes 4718592 | tf_op jit(solution)/shard_map/reshape;reshape | solution.py:141
  281.0 6.3 %copy.104 = bf16[2,128,64,72]{1,3,2,0:T(8,128)(2,1)} copy(bf16[2,128,64,72]{3,2,1,0:T(8,128)(2,1)} %reshape_reshape.17) | data formatting | bytes 4718592
  287.3 118.2 %while.30 = (s32[]{:T(128)}, f32[2,128,72]{1,2,0:T(8,128)S(1)}, bf16[2,128,64,2,72]{1,4,3,2,0:T(8,128)(2,1)}, s32[2,128]{1,0:T(2,128)S(1)}, f32[7,64,2,72]{3,1,2...) while((s32[]{:T(128)}, f32[2,128,72]{1,2,0:T(8,128)S(1)}, ...), condition=%wide.region_11.12_spmd.clone.clone, body=%wide.region_6.11_spmd.clone.clone.sunk | while | flops 3089797888 | bytes 120738984 | solution.py:163
  292.1 8.0 %copy.151 = f32[128,64,2,72]{0,3,2,1:T(8,128)} copy(f32[128,64,2,72]{3,1,2,0:T(8,128)} %gather_fusion) | data formatting | bytes 9437184 | tf_op jit(solution)/shard_map/while/body/eval_jaxpr/gather | solution.py:152
  304.4 8.1 %copy.152 = f32[128,64,2,72]{0,3,2,1:T(8,128)} copy(f32[128,64,2,72]{3,1,2,0:T(8,128)} %gather_fusion.1) | data formatting | bytes 9437184 | tf_op jit(solution)/shard_map/while/body/eval_jaxpr/gather | solution.py:151
  316.5 6.8 %subtract_reduce_fusion.4 = (f32[128,72]{0,1:T(8,128)S(1)}, f32[128,72]{0,1:T(8,128)S(1)}) fusion(f32[128,64,2,72]{0,3,2,1:T(8,128)S(1)} %copy-done.2, f32[128,64,2,72]{0,3,2,1:T(8,128)} %copy.152, f32[128,64,2,72]{0,3,2,1:T(8,128)S(1)} %fusion.358, bf16[2,128,64,2,72]{1,4,3,2,0:T(8,128)(2,1)} %get-tuple-element.545, s32[]{:T(128)} %get-tuple-element.533), kind=kOutput, calls=%fused_computation.13.clone.1 | convolution fusion | flops 1029860928 | bytes 16589312 | tf_op jit(solution)/shard_map/while/body/eval_jaxpr/dot_general | solution.py:64
  326.0 5.1 copy.153
  333.8 5.1 copy.154
  351.0 8.0 %copy.151 = f32[128,64,2,72]{0,3,2,1:T(8,128)} copy(f32[128,64,2,72]{3,1,2,0:T(8,128)} %gather_fusion) | data formatting | bytes 9437184 | tf_op jit(solution)/shard_map/while/body/eval_jaxpr/gather | solution.py:152
  363.3 8.1 %copy.152 = f32[128,64,2,72]{0,3,2,1:T(8,128)} copy(f32[128,64,2,72]{3,1,2,0:T(8,128)} %gather_fusion.1) | data formatting | bytes 9437184 | tf_op jit(solution)/shard_map/while/body/eval_jaxpr/gather | solution.py:151
  375.4 6.8 %subtract_reduce_fusion.4 = (f32[128,72]{0,1:T(8,128)S(1)}, f32[128,72]{0,1:T(8,128)S(1)}) fusion(f32[128,64,2,72]{0,3,2,1:T(8,128)S(1)} %copy-done.2, f32[128,64,2,72]{0,3,2,1:T(8,128)} %copy.152, f32[128,64,2,72]{0,3,2,1:T(8,128)S(1)} %fusion.358, bf16[2,128,64,2,72]{1,4,3,2,0:T(8,128)(2,1)} %get-tuple-element.545, s32[]{:T(128)} %get-tuple-element.533), kind=kOutput, calls=%fused_computation.13.clone.1 | convolution fusion | flops 1029860928 | bytes 16589312 | tf_op jit(solution)/shard_map/while/body/eval_jaxpr/dot_general | solution.py:64
  385.0 5.1 copy.153
  392.8 5.1 copy.154
  406.5 10.0 %all-to-all-start.2 = ((f32[32,1,512]{2,1,0:T(1,128)}), f32[32,1,512]{2,1,0:T(1,128)S(1)}, u32[]{:S(2)}, u32[]{:S(2)}) async-start(f32[32,1,512]{2,1,0:T(1,128)} %broadcast_in_dim.171), calls=%async_computation.2 | async-start | bytes 131072 | tf_op jit(solution)/shard_map/all_to_all | solution.py:23
  416.6 9.1 %all-to-all-done.2 = f32[32,1,512]{2,1,0:T(1,128)S(1)} async-done(((f32[32,1,512]{2,1,0:T(1,128)}), f32[32,1,512]{2,1,0:T(1,128)S(1)}, u32[]{:S(2)}, u32[]{:S(2)}) %all-to-all-start.2) | async-done | bytes 65568 | tf_op jit(solution)/shard_map/all_to_all | solution.py:23
  431.6 8.5 %all-to-all-done.3 = f32[32,1,512]{2,1,0:T(1,128)S(1)} async-done(((f32[32,1,512]{2,1,0:T(1,128)}), f32[32,1,512]{2,1,0:T(1,128)S(1)}, u32[]{:S(2)}, u32[]{:S(2)}) %all-to-all-start.3) | async-done | bytes 65568 | tf_op jit(solution)/shard_map/all_to_all | solution.py:23
  445.4 70.5 %while.31 = (s32[]{:T(128)}, f32[7,64,2,72]{3,0,2,1:T(8,128)S(1)}, f32[7,64,2,72]{3,0,2,1:T(8,128)}, f32[7,64,72]{2,0,1:T(8,128)}, f32[7,64,72]{2,0,1:T(8,128)},...) while((s32[]{:T(128)}, f32[7,64,2,72]{3,0,2,1:T(8,128)S(1)}, ...), condition=%wide.region_17.18_spmd.clone.clone, body=%wide.region_16.17_spmd.clone.clone.sunk | while | flops 3385679872 | bytes 105500520 | solution.py:225
  446.2 6.2 %fusion.382 = f32[128,64,2,72]{0,3,2,1:T(8,128)} fusion(bf16[2,128,64,2,72]{1,4,3,2,0:T(8,128)(2,1)} %get-tuple-element.581, s32[]{:T(128)} %get-tuple-element.564), kind=kOutput, calls=%fused_computation.103.clone.1 | convolution fusion | flops 1019262528 | bytes 7078400 | tf_op jit(solution)/shard_map/while/body/eval_jaxpr/dot_general | solution.py:64
  456.8 9.9 %fusion.387 = f32[7,64,2,72]{3,0,2,1:T(8,128)} fusion(f32[128,64,2,72]{0,3,2,1:T(8,128)} %fusion.382, f32[128,64,2,72]{0,3,2,1:T(8,128)} %fusion.383, f32[128,72]{0,1:T(8,128)S(1)} %convolution_negate_fusion.4, f32[128,72]{0,1:T(8,128)S(1)} %fusion.384, f32[7,64,2,72]{3,0,2,1:T(8,128)} %get-tuple-element.566, pred[]{:T(512)S(6)} %compare.18, ...), kind=kOutput, calls=%fused_computation.122.clone.1 | convolution fusion | flops 103938944 | bytes 10027521 | tf_op jit(solution)/shard_map/while/body/eval_jaxpr/bk,bsqf->ksqf/dot_general | solution.py:203
  466.8 5.3 fusion.386
  481.3 6.2 %fusion.382 = f32[128,64,2,72]{0,3,2,1:T(8,128)} fusion(bf16[2,128,64,2,72]{1,4,3,2,0:T(8,128)(2,1)} %get-tuple-element.581, s32[]{:T(128)} %get-tuple-element.564), kind=kOutput, calls=%fused_computation.103.clone.1 | convolution fusion | flops 1019262528 | bytes 7078400 | tf_op jit(solution)/shard_map/while/body/eval_jaxpr/dot_general | solution.py:64
  491.8 10.0 %fusion.387 = f32[7,64,2,72]{3,0,2,1:T(8,128)} fusion(f32[128,64,2,72]{0,3,2,1:T(8,128)} %fusion.382, f32[128,64,2,72]{0,3,2,1:T(8,128)} %fusion.383, f32[128,72]{0,1:T(8,128)S(1)} %convolution_negate_fusion.4, f32[128,72]{0,1:T(8,128)S(1)} %fusion.384, f32[7,64,2,72]{3,0,2,1:T(8,128)} %get-tuple-element.566, pred[]{:T(512)S(6)} %compare.18, ...), kind=kOutput, calls=%fused_computation.122.clone.1 | convolution fusion | flops 103938944 | bytes 10027521 | tf_op jit(solution)/shard_map/while/body/eval_jaxpr/bk,bsqf->ksqf/dot_general | solution.py:203
  501.8 5.3 fusion.386
  534.2 7.5 %all-to-all-done.4 = f32[8,7,1152]{2,1,0:T(8,128)S(1)} async-done(((f32[8,7,1152]{2,1,0:T(8,128)}), f32[8,7,1152]{2,1,0:T(8,128)S(1)}, u32[]{:S(2)}, u32[]{:S(2)}) %all-to-all-start.4) | async-done | bytes 258080 | tf_op jit(solution)/shard_map/all_to_all | solution.py:46
  (207 shorter events, 139.3 us)
Async XLA Ops:
  0.0 20.0 %copy-start.13 = (bf16[16,9216]{1,0:T(8,128)(2,1)S(1)}, bf16[16,9216]{1,0:T(8,128)(2,1)}, u32[]{:S(2)}) copy-start(bf16[16,9216]{1,0:T(8,128)(2,1)} %param.10) | copy-start | bytes 884740
  4.7 38.1 %all-to-all-start = ((s32[32,1,16]{2,1,0:T(1,128)}), s32[32,1,16]{2,1,0:T(1,128)S(1)}, u32[]{:S(2)}, u32[]{:S(2)}) async-start(s32[32,1,16]{2,1,0:T(1,128)} %bitcast.3), calls=%async_computation | async-start | bytes 32768 | tf_op jit(solution)/shard_map/all_to_all | solution.py:17
  25.7 5.0 copy-start.11
  34.2 3.5 copy-start.5
  42.8 10.4 %copy-start.12 = (bf16[7,9216]{1,0:T(8,128)(2,1)S(1)}, bf16[7,9216]{1,0:T(8,128)(2,1)}, u32[]{:S(2)}) copy-start(bf16[7,9216]{1,0:T(8,128)(2,1)} %param.14) | copy-start | bytes 387076
  42.8 166.2 %all-to-all-start.1 = ((bf16[32,8,13824]{2,1,0:T(8,128)(2,1)}), bf16[32,8,13824]{2,1,0:T(8,128)(2,1)}, u32[]{:S(2)}, u32[]{:S(2)}) async-start(bf16[32,8,13824]{2,1,0:T(8,128)(2,1)} %pad_maximum_fusion), calls=%async_computation.1 | async-start | bytes 14155776 | tf_op jit(solution)/shard_map/all_to_all | solution.py:17
  287.3 118.3 %copy-start.14 = (s32[256]{0:T(256)S(1)}, s32[256]{0:T(256)}, u32[]{:S(2)}) copy-start(s32[256]{0:T(256)} %eq.82) | copy-start | bytes 3076
  287.3 118.4 %copy-start.16 = (pred[256]{0:T(512)(128)(4,1)S(1)}, pred[256]{0:T(512)(128)(4,1)}, u32[]{:S(2)}) copy-start(pred[256]{0:T(512)(128)(4,1)} %ge.15) | copy-start | bytes 772
  287.3 129.3 %copy-start.15 = (s32[256,1]{0,1:T(1,128)S(1)}, s32[256,1]{0,1:T(1,128)}, u32[]{:S(2)}) copy-start(s32[256,1]{0,1:T(1,128)} %reshape.281) | copy-start | bytes 3076
  312.5 4.0 copy-start.2
  338.9 2.6 copy-start.3
  371.4 4.0 copy-start.2
  397.9 2.6 copy-start.3
  405.6 39.8 %copy-start.4 = (bf16[2,128,64,72]{1,3,2,0:T(8,128)(2,1)S(1)}, bf16[2,128,64,72]{1,3,2,0:T(8,128)(2,1)}, u32[]{:S(2)}) copy-start(bf16[2,128,64,72]{1,3,2,0:T(8,128)(2,1)} %get-tuple-element.587) | copy-start | bytes 7077892
  405.6 39.8 %copy-start.6 = (f32[7,64,2,72]{3,0,2,1:T(8,128)S(1)}, f32[7,64,2,72]{3,0,2,1:T(8,128)}, u32[]{:S(2)}) copy-start(f32[7,64,2,72]{3,0,2,1:T(8,128)} %custom-call) | copy-start | bytes 774148
  406.5 19.1 %all-to-all-start.2 = ((f32[32,1,512]{2,1,0:T(1,128)}), f32[32,1,512]{2,1,0:T(1,128)S(1)}, u32[]{:S(2)}, u32[]{:S(2)}) async-start(f32[32,1,512]{2,1,0:T(1,128)} %broadcast_in_dim.171), calls=%async_computation.2 | async-start | bytes 131072 | tf_op jit(solution)/shard_map/all_to_all | solution.py:23
  426.3 13.9 %all-to-all-start.3 = ((f32[32,1,512]{2,1,0:T(1,128)}), f32[32,1,512]{2,1,0:T(1,128)S(1)}, u32[]{:S(2)}, u32[]{:S(2)}) async-start(f32[32,1,512]{2,1,0:T(1,128)} %broadcast_in_dim.175), calls=%async_computation.3 | async-start | bytes 131072 | tf_op jit(solution)/shard_map/all_to_all | solution.py:23
  445.5 6.9 %copy-start.1 = (bf16[2,128,64,2,72]{1,4,3,2,0:T(8,128)(2,1)S(1)}, bf16[2,128,64,2,72]{1,4,3,2,0:T(8,128)(2,1)}, u32[]{:S(2)}) copy-start(bf16[2,128,64,2,72]{1,4,3,2,0:T(8,128)(2,1)} %get-tuple-element.581) | copy-start | bytes 14155780 | tf_op jit(solution)/shard_map/while
  452.5 14.3 %slice-start = ((s8[4718592]{0:T(1024)(128)(4,1)}), s8[524288]{0:T(1024)(128)(4,1)S(1)}, s32[]{:S(2)}) async-start(s8[4718592]{0:T(1024)(128)(4,1)} %bitcast.199), calls=%async_computation.6 | async-start | bytes 1048576 | tf_op jit(solution)/shard_map/while
  456.8 10.0 %slice-start.1 = ((s8[4718592]{0:T(1024)(128)(4,1)}), s8[4194304]{0:T(1024)(128)(4,1)S(1)}, s32[]{:S(2)}) async-start(s8[4718592]{0:T(1024)(128)(4,1)} %bitcast.199), calls=%async_computation.7 | async-start | bytes 8388608 | tf_op jit(solution)/shard_map/while
  456.8 10.0 %copy-start = (f32[128,64,2,72]{0,3,2,1:T(8,128)S(1)}, f32[128,64,2,72]{0,3,2,1:T(8,128)}, u32[]{:S(2)}) copy-start(f32[128,64,2,72]{0,3,2,1:T(8,128)} %fusion.383) | copy-start | bytes 14155780 | tf_op jit(solution)/shard_map/while
  473.3 3.9 copy-start.9
  477.2 2.7 copy-start.8
  480.6 6.9 %copy-start.1 = (bf16[2,128,64,2,72]{1,4,3,2,0:T(8,128)(2,1)S(1)}, bf16[2,128,64,2,72]{1,4,3,2,0:T(8,128)(2,1)}, u32[]{:S(2)}) copy-start(bf16[2,128,64,2,72]{1,4,3,2,0:T(8,128)(2,1)} %get-tuple-element.581) | copy-start | bytes 14155780 | tf_op jit(solution)/shard_map/while
  487.5 14.3 %slice-start = ((s8[4718592]{0:T(1024)(128)(4,1)}), s8[524288]{0:T(1024)(128)(4,1)S(1)}, s32[]{:S(2)}) async-start(s8[4718592]{0:T(1024)(128)(4,1)} %bitcast.199), calls=%async_computation.6 | async-start | bytes 1048576 | tf_op jit(solution)/shard_map/while
  491.8 10.0 %slice-start.1 = ((s8[4718592]{0:T(1024)(128)(4,1)}), s8[4194304]{0:T(1024)(128)(4,1)S(1)}, s32[]{:S(2)}) async-start(s8[4718592]{0:T(1024)(128)(4,1)} %bitcast.199), calls=%async_computation.7 | async-start | bytes 8388608 | tf_op jit(solution)/shard_map/while
  491.8 10.0 %copy-start = (f32[128,64,2,72]{0,3,2,1:T(8,128)S(1)}, f32[128,64,2,72]{0,3,2,1:T(8,128)}, u32[]{:S(2)}) copy-start(f32[128,64,2,72]{0,3,2,1:T(8,128)} %fusion.383) | copy-start | bytes 14155780 | tf_op jit(solution)/shard_map/while
  507.1 2.5 copy-start.7
  508.3 3.9 copy-start.9
  512.3 2.7 copy-start.8
  519.6 10.9 %all-to-all-start.5 = ((f32[8,7,576]{2,1,0:T(8,128)}), f32[8,7,576]{2,1,0:T(8,128)S(1)}, u32[]{:S(2)}, u32[]{:S(2)}) async-start(f32[8,7,576]{2,1,0:T(8,128)} %bitcast.144), calls=%async_computation.5 | async-start | bytes 327680 | tf_op jit(solution)/shard_map/all_to_all | solution.py:46
  530.5 11.2 %all-to-all-start.4 = ((f32[8,7,1152]{2,1,0:T(8,128)}), f32[8,7,1152]{2,1,0:T(8,128)S(1)}, u32[]{:S(2)}, u32[]{:S(2)}) async-start(f32[8,7,1152]{2,1,0:T(8,128)} %copy.111), calls=%async_computation.4 | async-start | bytes 589824 | tf_op jit(solution)/shard_map/all_to_all | solution.py:46
  (3 other events, 3.9 us)
where the time goes:
time: 553 us; the launch traced here: 543 us
  local copies, waits for them, and re-layouts  187 us (34%)
  waiting for transfers between devices  177 us (32%)
  matrix products  112 us (20%)
  starting transfers between devices  44 us (8%)
  other arithmetic  19.7 us (4%)
    all_to_all x2, waiting for transfers between devices, sent_together(): lax.all_to_all(both, axis, split_axis=split_dim, concat_axis=concat_dim,...  150 us
    dot_general x12, matrix products, forward_wave(): real_part = jnp.matmul(values, cos_table, precision=lax.Precision.HIGHEST)  38.7 us
    another operation x1, local copies, waits for them, and re-layouts, on_device(): row_weighted.reshape(block_count, block_size, shells, 2, angles)  35 us
    dot_general x12, matrix products, forward_wave(): imag_part = -jnp.matmul(values, sin_table, precision=lax.Precision.HIGHEST)  25.9 us
    gather x4, local copies, waits for them, and re-layouts, score_block(): match_real = ref_real[safe_class]  24.8 us
    gather x4, local copies, waits for them, and re-layouts, score_block(): match_imag = ref_imag[safe_class]  24.7 us
    unnamed x22, local copies, waits for them, and re-layouts  24.2 us
    all_to_all x2, starting transfers between devices, sent_together(): lax.all_to_all(both, axis, split_axis=split_dim, concat_axis=concat_dim,...  21.5 us
  transfers between devices with their start and end apart: 6, of which 5 were waited for; matrix products, arithmetic and copies ran while one was open for 7% of the time, Pallas kernels for 0%

commit v1 on v0

v1 whole, which is shorter than its diff:
```python
import jax
import jax.numpy as jnp
import numpy as np
from jax import lax
from jax.experimental import pallas as pl
from jax.experimental.pallas import tpu as pltpu
from jax.sharding import PartitionSpec as P

TOP = 4
NA = 72
HALF = 64
LANES = 128
PITCH = 16
SHELLS = 8
PAIR = 2 * NA
IMG_W = SHELLS * PAIR
CTF_W = SHELLS * NA
ROW_W = IMG_W + CTF_W
SEND_W = 1792
FREQS = NA // 2 + 1
TOPPAD = 112
TABLE = 384

bf16 = jnp.bfloat16
f32 = jnp.float32


def split3(x):
    x = np.asarray(x, np.float32)
    hi = x.astype(bf16)
    rest = x - hi.astype(np.float32)
    mid = rest.astype(bf16)
    low = (rest - mid.astype(np.float32)).astype(bf16)
    return np.stack([hi, mid, low])


def make_tables():
    freq = np.arange(FREQS)
    angle = np.arange(NA)
    phase = (freq[None, :] * angle[:, None]) % NA * (2.0 * np.pi / NA)
    cos, sin = np.cos(phase), np.sin(phase)
    weight = np.where((freq == 0) | (freq == NA // 2), 1.0, 2.0) / NA
    forward = np.zeros((TABLE, 2 * LANES))
    inverse = np.zeros((TABLE, 2 * LANES))
    even = np.zeros((TABLE, 2 * LANES))
    odd = np.zeros((TABLE, 2 * LANES))
    both = np.zeros((LANES, 2 * LANES))
    logit = np.zeros((2 * LANES, LANES))
    for part in range(2):
        rows = slice(TOPPAD + part * NA, TOPPAD + part * NA + NA)
        first = slice(TOPPAD, TOPPAD + NA)
        re = slice(part * HALF, part * HALF + FREQS)
        im = slice(LANES + part * HALF, LANES + part * HALF + FREQS)
        forward[rows, re], forward[rows, im] = cos, -sin
        inverse[rows, re], inverse[rows, im] = cos * weight, -sin * weight
        side = odd if part else even
        side[first, re], side[first, im] = -0.5 * cos, 0.5 * sin
        both[:NA, re], both[:NA, im] = cos, -sin
        logit[re, :NA], logit[im, :NA] = (cos * weight).T, (-sin * weight).T
    lane = np.arange(IMG_W)
    source = NA * (lane // PAIR) + lane % NA
    spread = (np.arange(CTF_W)[:, None] == source[None, :]).astype(bf16)
    return (
        split3(forward),
        np.stack([split3(even), split3(odd)]),
        split3(inverse)[:2],
        split3(both),
        logit.astype(np.float32),
        spread,
    )


def dot(a, b):
    return lax.dot_general(a, b, (((1,), (0,)), ((), ())), preferred_element_type=f32)


def dot_t(a, b):
    return lax.dot_general(a, b, (((1,), (1,)), ((), ())), preferred_element_type=f32)


def window(table_ref, lead, index):
    start = TOPPAD - 16 * index
    return table_ref[(*lead, slice(start, start + 2 * LANES), slice(None))]


def pack_kernel(img_ref, images, ctf, classes, place, refs, wsend, rsend):
    rows = []
    lane = lax.broadcasted_iota(jnp.int32, (16, 64), 1)
    for j in range(TOP):
        hit = classes[:, j : j + 1] == lax.broadcasted_iota(jnp.int32, (16, 224), 1)
        rows.append(jnp.sum(jnp.where(hit, place[...], 0), axis=1, keepdims=True))
    listed = jnp.zeros((16, 64), f32)
    for j in range(TOP):
        listed = jnp.where(lane == j, rows[j].astype(f32), listed)
    tail = listed.astype(bf16)
    for d in range(8):
        wsend[d, :, :IMG_W] = images[:, d * IMG_W : (d + 1) * IMG_W]
        wsend[d, :, IMG_W:] = jnp.concatenate(
            [ctf[:, d * CTF_W : (d + 1) * CTF_W], tail], axis=1
        )
    start = pl.multiple_of(img_ref[0] * IMG_W, LANES)
    mine = refs[:, pl.ds(start, IMG_W)].astype(f32)
    mine = jnp.concatenate([mine, jnp.zeros((1, IMG_W), f32)], axis=0).astype(bf16)
    for o in range(32):
        rsend[o] = mine


def weigh_kernel(recv, inv, spread, fwd, wre, wim):
    ctf = recv[:, IMG_W:ROW_W]
    ctf32 = ctf.astype(f32)
    power = (ctf32 * (ctf32 * inv[:, IMG_W:ROW_W])).astype(bf16)
    power = jnp.concatenate([power, jnp.zeros((LANES, 64), bf16)], axis=1)
    scale = dot(ctf, spread[...]) * inv[:, :IMG_W]
    weighted = (recv[:, :IMG_W].astype(f32) * scale).astype(bf16)
    count = recv.shape[0]
    for s in range(SHELLS + 4):
        if s < SHELLS:
            x = weighted[:, LANES * s : LANES * s + 2 * LANES]
            index = s
        else:
            index = s - SHELLS
            x = power[:, LANES * index : LANES * index + 2 * LANES]
        y = dot(x, window(fwd, (0,), index))
        y += dot(x, window(fwd, (1,), index))
        y += dot(x, window(fwd, (2,), index))
        wre[pl.ds(s, count, stride=PITCH), :] = y[:, :LANES]
        wim[pl.ds(s, count, stride=PITCH), :] = y[:, LANES:]
    zero = jnp.zeros((count, LANES), f32)
    for s in range(SHELLS + 4, PITCH):
        wre[pl.ds(s, count, stride=PITCH), :] = zero
        wim[pl.ds(s, count, stride=PITCH), :] = zero


def score_kernel(idx, recv, fwd, side, logit, wre, wim, out, rre, rim, pq):
    count = 256
    raw32 = recv[...].astype(f32).reshape(count, IMG_W)
    raw = raw32.astype(bf16)
    square = raw32 * raw32
    shifted = jnp.concatenate([square[:, NA:], square[:, :NA]], axis=1)
    power = (square + shifted).astype(bf16)
    for s in range(SHELLS):
        x = raw[:, LANES * s : LANES * s + 2 * LANES]
        y = dot(x, window(fwd, (0,), s))
        y += dot(x, window(fwd, (1,), s))
        y += dot(x, window(fwd, (2,), s))
        rre[pl.ds(s, count, stride=PITCH), :] = y[:, :LANES]
        rim[pl.ds(s, count, stride=PITCH), :] = y[:, LANES:]
    for j in range(SHELLS // 2):
        y = jnp.zeros((count, 2 * LANES), f32)
        for parity in range(2):
            s = 2 * j + parity
            x = power[:, LANES * s : LANES * s + 2 * LANES]
            for k in range(3):
                y += dot(x, window(side, (parity, k), s))
        rre[pl.ds(SHELLS + j, count, stride=PITCH), :] = y[:, :LANES]
        rim[pl.ds(SHELLS + j, count, stride=PITCH), :] = y[:, LANES:]
    zero = jnp.zeros((count, LANES), f32)
    for s in range(SHELLS + 4, PITCH):
        rre[pl.ds(s, count, stride=PITCH), :] = zero
        rim[pl.ds(s, count, stride=PITCH), :] = zero

    def block(b, carry):
        rows = [[[], []] for _ in range(TOP)]
        for u in range(8):
            i = b * 8 + u
            at = pl.multiple_of(i * PITCH, PITCH)
            a_re = wre[pl.ds(at, PITCH), :]
            a_im = wim[pl.ds(at, PITCH), :]
            for j in range(TOP):
                t = pl.multiple_of(idx[i * TOP + j] * PITCH, PITCH)
                b_re = rre[pl.ds(t, PITCH), :]
                b_im = rim[pl.ds(t, PITCH), :]
                p = a_re * b_re + a_im * b_im
                q = a_im * b_re - a_re * b_im
                rows[j][0].append(jnp.sum(p, axis=0, keepdims=True))
                rows[j][1].append(jnp.sum(q, axis=0, keepdims=True))
        at = pl.multiple_of(b * 8, 8)
        for j in range(TOP):
            pq[j, pl.ds(at, 8), :LANES] = jnp.concatenate(rows[j][0], axis=0)
            pq[j, pl.ds(at, 8), LANES:] = jnp.concatenate(rows[j][1], axis=0)
        return carry

    lax.fori_loop(0, 16, block, 0)
    for j in range(TOP):
        out[:, LANES * j : LANES * j + LANES] = lax.dot_general(
            pq[j],
            logit[...],
            (((1,), (0,)), ((), ())),
            precision=lax.Precision.HIGHEST,
            preferred_element_type=f32,
        )


def softmax_kernel(parts, out):
    logits = parts[0]
    for k in range(1, 8):
        logits += parts[k]
    lane = lax.broadcasted_iota(jnp.int32, logits.shape, 1)
    valid = lane % LANES < NA
    logits = jnp.where(valid, logits, -jnp.inf)
    highest = jnp.max(logits, axis=1, keepdims=True)
    e = jnp.exp(logits - highest)
    posterior = (e / jnp.sum(e, axis=1, keepdims=True)).astype(bf16)
    for k in range(8):
        out[k] = posterior


def gather_kernel(idx, post, both, inverse, wre, wim, out, gre, gim, are, aim, total):
    for j in range(TOP):
        x = post[:, LANES * j : LANES * j + LANES]
        y = dot(x, both[0]) + dot(x, both[1]) + dot(x, both[2])
        gre[j] = y[:, :LANES]
        gim[j] = y[:, LANES:]
    are[...] = jnp.zeros_like(are)
    aim[...] = jnp.zeros_like(aim)

    def block(b, carry):
        for u in range(4):
            i = b * 4 + u
            at = pl.multiple_of(i * PITCH, PITCH)
            a_re = wre[pl.ds(at, PITCH), :]
            a_im = wim[pl.ds(at, PITCH), :]
            places, sums = [], []
            for j in range(TOP):
                t = pl.multiple_of(idx[i * TOP + j] * PITCH, PITCH)
                g_re = gre[j, pl.ds(i, 1), :]
                g_im = gim[j, pl.ds(i, 1), :]
                places.append(t)
                sums.append(
                    (
                        are[pl.ds(t, PITCH), :] + (a_re * g_re + a_im * g_im),
                        aim[pl.ds(t, PITCH), :] + (a_im * g_re - a_re * g_im),
                    )
                )
            for j in range(TOP):
                are[pl.ds(places[j], PITCH), :] = sums[j][0]
                aim[pl.ds(places[j], PITCH), :] = sums[j][1]
        return carry

    lax.fori_loop(0, 32, block, 0)
    count = 256
    total[...] = jnp.zeros_like(total)
    for s in range(SHELLS + 4):
        index = s if s < SHELLS else s - SHELLS
        base = LANES * s if s < SHELLS else IMG_W + LANES * index
        x = jnp.concatenate(
            [are[pl.ds(s, count, stride=PITCH), :], aim[pl.ds(s, count, stride=PITCH), :]], axis=1
        )
        hi = x.astype(bf16)
        low = (x - hi.astype(f32)).astype(bf16)
        t_hi, t_low = window(inverse, (0,), index), window(inverse, (1,), index)
        y = dot_t(hi, t_hi) + dot_t(low, t_hi) + dot_t(hi, t_low)
        total[:, base : base + 2 * LANES] += y
    out[...] = total[...].reshape(32, 8, SEND_W).astype(bf16)


def final_kernel(parts, spread, out):
    total = parts[0].astype(f32)
    for k in range(1, 32):
        total += parts[k].astype(f32)
    below = lax.dot_general(
        total[:, IMG_W:ROW_W] + 1.0,
        spread[...].astype(f32),
        (((1,), (0,)), ((), ())),
        precision=lax.Precision.HIGHEST,
        preferred_element_type=f32,
    )
    out[...] = (total[:, :IMG_W] / below)[:7]


VM = pl.BlockSpec(memory_space=pltpu.VMEM)
SM = pl.BlockSpec(memory_space=pltpu.SMEM)
PARAMS = pltpu.CompilerParams(vmem_limit_bytes=56 * 1024 * 1024)


def on_device(images, ctf, classes, class_place, references, sigma2):
    fwd, side, inverse, both, logit, spread = make_tables()
    img = lax.axis_index("img")
    wsend, rsend = pl.pallas_call(
        pack_kernel,
        out_shape=(
            jax.ShapeDtypeStruct((8, 16, SEND_W), bf16),
            jax.ShapeDtypeStruct((32, 8, IMG_W), bf16),
        ),
        in_specs=[SM, VM, VM, VM, VM, VM],
        out_specs=(VM, VM),
        compiler_params=PARAMS,
        name="pack",
    )(img.reshape(1), images, ctf, classes, class_place.reshape(1, -1), references)
    wrecv = lax.all_to_all(wsend, "img", 0, 0, tiled=True).reshape(128, SEND_W)
    rrecv = lax.all_to_all(rsend, "cls", 0, 0, tiled=True)
    table_rows = wrecv[:, ROW_W : ROW_W + TOP].astype(jnp.int32)
    idx = (table_rows // 7 * 8 + table_rows % 7).reshape(-1)
    inv = 1.0 / lax.dynamic_slice(sigma2, (img * SHELLS,), (SHELLS,))
    inv = jnp.concatenate([jnp.repeat(inv, PAIR), jnp.repeat(inv, NA)]).reshape(1, ROW_W)
    hat = jax.ShapeDtypeStruct((128 * PITCH, LANES), f32)
    wre, wim = pl.pallas_call(
        weigh_kernel,
        out_shape=(hat, hat),
        in_specs=[VM] * 4,
        out_specs=(VM, VM),
        compiler_params=PARAMS,
        name="weigh",
    )(wrecv, inv, spread, fwd)
    partial = pl.pallas_call(
        score_kernel,
        out_shape=jax.ShapeDtypeStruct((128, TOP * LANES), f32),
        in_specs=[SM] + [VM] * 6,
        out_specs=VM,
        scratch_shapes=[
            pltpu.VMEM((256 * PITCH, LANES), f32),
            pltpu.VMEM((256 * PITCH, LANES), f32),
            pltpu.VMEM((TOP, 128, 2 * LANES), f32),
        ],
        compiler_params=PARAMS,
        name="score",
    )(idx, rrecv, fwd, side, logit, wre, wim)
    parts = lax.all_to_all(partial.reshape(8, 16, TOP * LANES), "img", 0, 0, tiled=True)
    post = pl.pallas_call(
        softmax_kernel,
        out_shape=jax.ShapeDtypeStruct((8, 16, TOP * LANES), bf16),
        in_specs=[VM],
        out_specs=VM,
        compiler_params=PARAMS,
        name="softmax",
    )(parts)
    post = lax.all_to_all(post, "img", 0, 0, tiled=True).reshape(128, TOP * LANES)
    sums = pl.pallas_call(
        gather_kernel,
        out_shape=jax.ShapeDtypeStruct((32, 8, SEND_W), bf16),
        in_specs=[SM] + [VM] * 5,
        out_specs=VM,
        scratch_shapes=[
            pltpu.VMEM((TOP, 128, LANES), f32),
            pltpu.VMEM((TOP, 128, LANES), f32),
            pltpu.VMEM((256 * PITCH, LANES), f32),
            pltpu.VMEM((256 * PITCH, LANES), f32),
            pltpu.VMEM((256, SEND_W), f32),
        ],
        compiler_params=PARAMS,
        name="gather",
    )(idx, post, both, inverse, wre, wim)
    arrived = lax.all_to_all(sums, "cls", 0, 0, tiled=True)
    return pl.pallas_call(
        final_kernel,
        out_shape=jax.ShapeDtypeStruct((7, IMG_W), f32),
        in_specs=[VM, VM],
        out_specs=VM,
        compiler_params=PARAMS,
        name="final",
    )(arrived, spread)


def solution(mesh):
    in_specs = (
        P(("cls", "img"), None),
        P(("cls", "img"), None),
        P(("cls", "img"), None),
        P(),
        P("cls", None),
        P(),
    )
    return jax.shard_map(
        on_device, mesh=mesh, in_specs=in_specs, out_specs=P("cls", "img"), check_vma=False
    )
```

time: 553 us -> 122 us (0.22); the launches traced: 543 us -> 121 us
  local copies, waits for them, and re-layouts: 187 us -> 3.78 us
  waiting for transfers between devices: 177 us -> 12.3 us
  matrix products: 112 us -> 0 us
  blocking collectives: 0 us -> 66.5 us
  starting transfers between devices: 44 us -> 11.2 us
  Pallas kernels: 0 us -> 27.4 us
  other arithmetic: 19.7 us -> 0.24 us
    all_to_all x6 -> x1, waiting for transfers between devices: 177 us -> 12.3 us  [on_device(): rrecv = lax.all_to_all(rsend, 'cls', 0, 0, tiled=True)]
    dot_general x40 -> x0, matrix products: 112 us -> none  [the longest x12 38.7 us: forward_wave(): real_part = jnp.matmul(values, cos_table, precision=lax.Precision.HIGHEST)]
    gather x21 -> x0, local copies, waits for them, and re-layouts: 95.6 us -> none  [the longest x4 24.8 us: score_block(): match_real = ref_real[safe_class]]
    all_to_all x0 -> x4, blocking collectives: none -> 66.5 us  [the longest x1 30.7 us: on_device(): arrived = lax.all_to_all(sums, 'cls', 0, 0, tiled=True)]
    another operation x6 -> x0, local copies, waits for them, and re-layouts: 47.7 us -> none  [the longest x1 35 us: on_device(): row_weighted.reshape(block_count, block_size, shells, 2, angles)]
    all_to_all x6 -> x1, starting transfers between devices: 44 us -> 11.2 us  [on_device(): rrecv = lax.all_to_all(rsend, 'cls', 0, 0, tiled=True)]
    pallas_call x0 -> x6, Pallas kernels: none -> 27.4 us  [the longest x1 8.67 us: on_device(): pl.pallas_call(score_kernel, out_shape=jax.ShapeDtypeStruct((128, TOP * L...]
    unnamed x22 -> x7, local copies, waits for them, and re-layouts: 24.2 us -> 2.19 us
  transfers between devices with their start and end apart: 6 -> 1, of which waited for: 5 -> 1; matrix products, arithmetic and copies ran while one was open for 7% -> 2% of each run, Pallas kernels for 0% -> 4%
where the time goes in v1:
time: 122 us; the launch traced here: 121 us
  blocking collectives  66.5 us (55%)
  Pallas kernels  27.4 us (22%)
  waiting for transfers between devices  12.3 us (10%)
  starting transfers between devices  11.2 us (9%)
  local copies, waits for them, and re-layouts  3.78 us (3%)
    all_to_all x1, blocking collectives, on_device(): arrived = lax.all_to_all(sums, 'cls', 0, 0, tiled=True)  30.7 us
    all_to_all x1, blocking collectives, on_device(): wrecv = lax.all_to_all(wsend, 'img', 0, 0, tiled=True).reshape(128, SEND_W)  14.2 us
    all_to_all x1, waiting for transfers between devices, on_device(): rrecv = lax.all_to_all(rsend, 'cls', 0, 0, tiled=True)  12.3 us
    all_to_all x1, blocking collectives, on_device(): lax.all_to_all(partial.reshape(8, 16, TOP * LANES), 'img', 0, 0, tiled=True)  11.6 us
    all_to_all x1, starting transfers between devices, on_device(): rrecv = lax.all_to_all(rsend, 'cls', 0, 0, tiled=True)  11.2 us
    all_to_all x1, blocking collectives, on_device(): lax.all_to_all(post, 'img', 0, 0, tiled=True).reshape(128, TOP * LANES)  10.1 us
    pallas_call x1, Pallas kernels, on_device(): pl.pallas_call(score_kernel, out_shape=jax.ShapeDtypeStruct((128, TOP * L...  8.67 us
    pallas_call x1, Pallas kernels, on_device(): pl.pallas_call(gather_kernel, out_shape=jax.ShapeDtypeStruct((32, 8, SEND...  6.59 us
  transfers between devices with their start and end apart: 1, of which 1 were waited for; matrix products, arithmetic and copies ran while one was open for 2% of the time, Pallas kernels for 4%

profile of v1, /device:TPU:32, one launch (start us, length us, event | category | flops | bytes accessed | tf_op | source)
XLA Modules:
  0.0 121.4 jit_solution(14977299273670114073)
XLA Ops:
  0.0 1.4 %copy.14.classes = s32[16,4]{1,0:T(8,128)} copy(s32[16,4]{0,1:T(4,128)} %param.14) | data formatting | bytes 512 | tf_op args[2]
  1.4 0.0 copy-start.2
  1.4 2.3 %pack.1 = (bf16[8,16,1792]{2,1,0:T(8,128)(2,1)}, bf16[32,8,1152]{2,1,0:T(8,128)(2,1)}) custom-call(s32[1]{0:T(128)} %bitcast.img_ref, bf16[16,9216]{1,0:T(8,128)(2,1)} %images.1, bf16[16,4608]{1,0:T(8,128)(2,1)} %ctf.1, s32[16,4]{1,0:T(8,128)} %copy.14.classes, s32[1,224]{1,0:T(1,128)} %bitcast.9, bf16[7,9216]{1,0:T(8,128)(2,1)} %refs.1), custom_call_target="tpu_custom_call" | custom-call | tf_op jit(solution)/shard_map/pack/pallas_call | solution.py:279
  3.7 14.2 %all_to_all.25 = bf16[8,16,1792]{2,1,0:T(8,128)(2,1)S(1)} all-to-all(bf16[8,16,1792]{2,1,0:T(8,128)(2,1)} %get-tuple-element.9), channel_id=1, replica_groups=mesh['cls'=32,'img'=8] {'img'}, dimensions={0} | all-to-all | bytes 917504 | tf_op jit(solution)/shard_map/all_to_all | solution.py:290
  17.8 0.0 copy-start.1
  17.8 11.2 %all-to-all-start.1 = ((bf16[32,8,1152]{2,1,0:T(8,128)(2,1)}), bf16[32,8,1152]{2,1,0:T(8,128)(2,1)S(1)}, u32[]{:S(2)}, u32[]{:S(2)}) async-start(bf16[32,8,1152]{2,1,0:T(8,128)(2,1)} %get-tuple-element.10), calls=%async_computation.1 | async-start | bytes 1179648 | tf_op jit(solution)/shard_map/all_to_all | solution.py:291
  29.0 0.0 copy-done.2
  29.1 0.1 dynamic-slice_divide_fusion
  29.1 0.1 broadcast_in_dim.7
  29.2 0.1 reshape.32
  29.3 0.1 broadcast_in_dim.6
  29.3 0.1 reshape.31
  29.5 0.6 reshape.33.inv
  30.1 0.2 fusion.4
  30.2 0.7 reshape.30.idx
  30.9 0.0 copy-done.1
  30.9 4.5 %weigh.1 = (f32[2048,128]{1,0:T(8,128)}, f32[2048,128]{1,0:T(8,128)}) custom-call(bf16[128,1792]{1,0:T(8,128)(2,1)} %bitcast.6, f32[1,1728]{1,0:T(1,128)} %reshape.33.inv, bf16[576,1152]{1,0:T(8,128)(2,1)} %constant.44.clone.spread, bf16[3,384,256]{2,1,0:T(8,128)(2,1)} %constant.45.clone.fwd), custom_call_target="tpu_custom_call" | custom-call | tf_op jit(solution)/shard_map/weigh/pallas_call | solution.py:297
  35.4 12.3 %all-to-all-done.1.recv = bf16[32,8,1152]{2,1,0:T(8,128)(2,1)S(1)} async-done(((bf16[32,8,1152]{2,1,0:T(8,128)(2,1)}), bf16[32,8,1152]{2,1,0:T(8,128)(2,1)S(1)}, u32[]{:S(2)}, u32[]{:S(2)}) %all-to-all-start.1) | async-done | bytes 589856 | tf_op jit(solution)/shard_map/all_to_all | solution.py:291
  47.7 0.0 copy-start
  47.7 0.8 copy-done
  48.5 8.7 %score.1 = f32[128,512]{1,0:T(8,128)} custom-call(s32[512]{0:T(512)} %reshape.30.idx, bf16[32,8,1152]{2,1,0:T(8,128)(2,1)} %copy-done, bf16[3,384,256]{2,1,0:T(8,128)(2,1)} %constant.45.clone.fwd, bf16[2,3,384,256]{3,2,1,0:T(8,128)(2,1)} %constant.46.clone.side, f32[256,128]{1,0:T(8,128)} %constant.47.clone.logit, f32[2048,128]{1,0:T(8,128)} %get-tuple-element.11.wre, ...), custom_call_target="tpu_custom_call" | custom-call | tf_op jit(solution)/shard_map/score/pallas_call | solution.py:305
  57.2 11.6 %all_to_all.26.parts = f32[8,16,512]{2,1,0:T(8,128)} all-to-all(f32[8,16,512]{2,1,0:T(8,128)} %bitcast.7), channel_id=1, replica_groups=mesh['cls'=32,'img'=8] {'img'}, dimensions={0} | all-to-all | bytes 524288 | tf_op jit(solution)/shard_map/all_to_all | solution.py:318
  68.8 1.8 %softmax.1 = bf16[8,16,512]{2,1,0:T(8,128)(2,1)} custom-call(f32[8,16,512]{2,1,0:T(8,128)} %all_to_all.26.parts), custom_call_target="tpu_custom_call" | custom-call | tf_op jit(solution)/shard_map/softmax/pallas_call | solution.py:319
  70.6 10.1 %all_to_all.27 = bf16[8,16,512]{2,1,0:T(8,128)(2,1)} all-to-all(bf16[8,16,512]{2,1,0:T(8,128)(2,1)} %softmax.1), channel_id=1, replica_groups=mesh['cls'=32,'img'=8] {'img'}, dimensions={0} | all-to-all | bytes 262144 | tf_op jit(solution)/shard_map/all_to_all | solution.py:327
  80.7 6.6 %gather.1 = bf16[32,8,1792]{2,1,0:T(8,128)(2,1)} custom-call(s32[512]{0:T(512)} %reshape.30.idx, bf16[128,512]{1,0:T(8,128)(2,1)} %bitcast.8, bf16[3,128,256]{2,1,0:T(8,128)(2,1)} %constant.48.clone.both, bf16[2,384,256]{2,1,0:T(8,128)(2,1)} %constant.49.clone.inverse, f32[2048,128]{1,0:T(8,128)} %get-tuple-element.11.wre, f32[2048,128]{1,0:T(8,128)} %get-tuple-element.12.wim), custom_call_target="tpu_custom_call" | custom-call | tf_op jit(solution)/shard_map/gather/pallas_call | solution.py:328
  87.3 30.7 %all_to_all.28.parts = bf16[32,8,1792]{2,1,0:T(8,128)(2,1)} all-to-all(bf16[32,8,1792]{2,1,0:T(8,128)(2,1)} %gather.1), channel_id=1, replica_groups=mesh['cls'=32,'img'=8] {'cls'}, dimensions={0} | all-to-all | bytes 1835008 | tf_op jit(solution)/shard_map/all_to_all | solution.py:343
  118.0 3.5 %final.1 = f32[7,1152]{1,0:T(8,128)} custom-call(bf16[32,8,1792]{2,1,0:T(8,128)(2,1)} %all_to_all.28.parts, bf16[576,1152]{1,0:T(8,128)(2,1)} %constant.44.clone.spread), custom_call_target="tpu_custom_call" | custom-call | tf_op jit(solution)/shard_map/final/pallas_call | solution.py:344
  (1 shorter events, 0.0 us)
Async XLA Ops:
  1.4 27.7 %copy-start.2 = (f32[64]{0:T(128)S(1)}, f32[64]{0:T(128)}, u32[]{:S(2)}) copy-start(f32[64]{0:T(128)} %param.17) | copy-start | bytes 772
  17.8 13.1 %copy-start.1 = (bf16[8,16,1792]{2,1,0:T(8,128)(2,1)}, bf16[8,16,1792]{2,1,0:T(8,128)(2,1)S(1)}, u32[]{:S(2)}) copy-start(bf16[8,16,1792]{2,1,0:T(8,128)(2,1)S(1)} %all_to_all.25) | copy-start | bytes 1376260
  17.8 29.9 %all-to-all-start.1 = ((bf16[32,8,1152]{2,1,0:T(8,128)(2,1)}), bf16[32,8,1152]{2,1,0:T(8,128)(2,1)S(1)}, u32[]{:S(2)}, u32[]{:S(2)}) async-start(bf16[32,8,1152]{2,1,0:T(8,128)(2,1)} %get-tuple-element.10), calls=%async_computation.1 | async-start | bytes 1179648 | tf_op jit(solution)/shard_map/all_to_all | solution.py:291
  47.7 0.8 copy-start

commit v2 on v1

v2 whole, which is shorter than its diff:
```python
import jax
import jax.numpy as jnp
import numpy as np
from jax import lax
from jax.experimental import pallas as pl
from jax.experimental.pallas import tpu as pltpu
from jax.sharding import Mesh
from jax.sharding import PartitionSpec as P

TOP = 4
NA = 72
HALF = 64
LANES = 128
PITCH = 8
SHELLS = 4
WINDOWS = 6
MEMBERS = 16
PARTICLES = 16 * MEMBERS
OWNERS = 32
TABLE_ROWS = 8 * OWNERS
PAIR = 2 * NA
IMG_W = SHELLS * PAIR
CTF_W = SHELLS * NA
REF_W = 640
ROW_W = IMG_W + CTF_W
SEND_W = 896
LOGIT_W = 384
FREQS = NA // 2 + 1
TOPPAD = 112
TABLE = 384
CLS = ("xh", "xl", "z")
GROUP = ("xl", "img")
DEVICES = ("xh", "xl", "z", "img")

bf16 = jnp.bfloat16
f32 = jnp.float32


def split3(x):
    x = np.asarray(x, np.float32)
    hi = x.astype(bf16)
    rest = x - hi.astype(np.float32)
    mid = rest.astype(bf16)
    low = (rest - mid.astype(np.float32)).astype(bf16)
    return np.stack([hi, mid, low])


def make_tables():
    freq = np.arange(FREQS)
    angle = np.arange(NA)
    phase = (freq[None, :] * angle[:, None]) % NA * (2.0 * np.pi / NA)
    cos, sin = np.cos(phase), np.sin(phase)
    weight = np.where((freq == 0) | (freq == NA // 2), 1.0, 2.0) / NA
    forward = np.zeros((TABLE, 2 * LANES))
    inverse = np.zeros((TABLE, 2 * LANES))
    side = np.zeros((2, TABLE, 2 * LANES))
    both = np.zeros((2, TABLE, 2 * LANES))
    logit = np.zeros((2 * LANES, LANES))
    first = slice(TOPPAD, TOPPAD + NA)
    for part in range(2):
        rows = slice(TOPPAD + part * NA, TOPPAD + part * NA + NA)
        re = slice(part * HALF, part * HALF + FREQS)
        im = slice(LANES + part * HALF, LANES + part * HALF + FREQS)
        forward[rows, re], forward[rows, im] = cos, -sin
        inverse[rows, re], inverse[rows, im] = cos * weight, -sin * weight
        side[part, first, re], side[part, first, im] = -0.5 * cos, 0.5 * sin
        for second in range(2):
            at = slice(TOPPAD + second * NA, TOPPAD + second * NA + NA)
            both[second, at, re], both[second, at, im] = cos, -sin
        logit[re, :NA], logit[im, :NA] = (cos * weight).T, (-sin * weight).T
    lane = np.arange(SEND_W)
    source = np.where(lane < IMG_W, IMG_W + NA * (lane // PAIR) + lane % NA, lane) - 512
    spread = (np.arange(384)[:, None] == source[None, :]) & (lane < ROW_W)[None, :]
    below = (np.arange(384)[:, None] == source[None, :]) & (lane < IMG_W)[None, :]
    return (
        split3(forward),
        np.stack([split3(side[0]), split3(side[1])]),
        split3(inverse)[:2],
        np.stack([split3(both[0])[:2], split3(both[1])[:2]]),
        logit.astype(np.float32),
        spread.astype(bf16),
        below[:, :REF_W].astype(bf16),
    )


def dot(a, b):
    return lax.dot_general(a, b, (((1,), (0,)), ((), ())), preferred_element_type=f32)


def dot_t(a, b):
    return lax.dot_general(a, b, (((1,), (1,)), ((), ())), preferred_element_type=f32)


def dot_exact(a, b):
    return lax.dot_general(
        a,
        b,
        (((1,), (0,)), ((), ())),
        precision=lax.Precision.HIGHEST,
        preferred_element_type=f32,
    )


def window(table_ref, lead, index):
    start = TOPPAD - 16 * index
    return table_ref[(*lead, slice(start, start + 2 * LANES), slice(None))]


def lanes_of(x, index):
    return x[:, LANES * index : LANES * index + 2 * LANES]


def pack_kernel(at_ref, images, ctf, classes, place, refs, wsend, rsend):
    lane = lax.broadcasted_iota(jnp.int32, (16, SEND_W - ROW_W), 1)
    listed = jnp.zeros((16, SEND_W - ROW_W), f32)
    for j in range(TOP):
        hit = classes[:, j : j + 1] == lax.broadcasted_iota(jnp.int32, (16, 224), 1)
        row = jnp.sum(jnp.where(hit, place[...], 0), axis=1, keepdims=True)
        listed = jnp.where(lane == j, row.astype(f32), listed)
    tail = listed.astype(bf16)
    for h in range(2):
        for i in range(8):
            shell = i * 8 + h * SHELLS
            wsend[h * 8 + i] = jnp.concatenate(
                [
                    images[:, shell * PAIR : shell * PAIR + IMG_W],
                    ctf[:, shell * NA : shell * NA + CTF_W],
                    tail,
                ],
                axis=1,
            )
    start = pl.multiple_of(at_ref[0] * 2 * IMG_W, LANES)
    mine = refs[:, pl.ds(start, 2 * IMG_W)].astype(f32)
    for h in range(2):
        half = mine[:, h * IMG_W : (h + 1) * IMG_W]
        half = jnp.concatenate([half, jnp.zeros((7, REF_W - IMG_W), f32)], axis=1)
        half = jnp.concatenate([half, jnp.zeros((1, REF_W), f32)], axis=0).astype(bf16)
        for o in range(OWNERS):
            if (o // 8) % 2 == h:
                rsend[o] = half


def weigh_kernel(recv, inv, spread, fwd, wre, wim):
    scale = dot(recv[:, 512:], spread[...]) * inv[...]
    weighted = (recv[...].astype(f32) * scale).astype(bf16)
    for s in range(WINDOWS):
        x = lanes_of(weighted, s)
        y = sum(dot(x, window(fwd, (k,), s)) for k in range(3))
        wre[pl.ds(s, PARTICLES, stride=PITCH), :] = y[:, :LANES]
        wim[pl.ds(s, PARTICLES, stride=PITCH), :] = y[:, LANES:]
    zero = jnp.zeros((PARTICLES, LANES), f32)
    for s in range(WINDOWS, PITCH):
        wre[pl.ds(s, PARTICLES, stride=PITCH), :] = zero
        wim[pl.ds(s, PARTICLES, stride=PITCH), :] = zero


def score_kernel(idx, recv, fwd, side, logit, wre, wim, out, rre, rim, pq):
    raw32 = recv[...].astype(f32).reshape(TABLE_ROWS, REF_W)
    raw = raw32.astype(bf16)
    square = raw32 * raw32
    shifted = jnp.concatenate([square[:, NA:], square[:, :NA]], axis=1)
    power = (square + shifted).astype(bf16)
    for s in range(SHELLS):
        y = sum(dot(lanes_of(raw, s), window(fwd, (k,), s)) for k in range(3))
        rre[pl.ds(s, TABLE_ROWS, stride=PITCH), :] = y[:, :LANES]
        rim[pl.ds(s, TABLE_ROWS, stride=PITCH), :] = y[:, LANES:]
    for j in range(SHELLS // 2):
        y = sum(
            dot(lanes_of(power, 2 * j + parity), window(side, (parity, k), 2 * j + parity))
            for parity in range(2)
            for k in range(3)
        )
        rre[pl.ds(SHELLS + j, TABLE_ROWS, stride=PITCH), :] = y[:, :LANES]
        rim[pl.ds(SHELLS + j, TABLE_ROWS, stride=PITCH), :] = y[:, LANES:]
    zero = jnp.zeros((TABLE_ROWS, LANES), f32)
    for s in range(WINDOWS, PITCH):
        rre[pl.ds(s, TABLE_ROWS, stride=PITCH), :] = zero
        rim[pl.ds(s, TABLE_ROWS, stride=PITCH), :] = zero

    def block(b, carry):
        rows = [[[], []] for _ in range(TOP)]
        for u in range(8):
            i = b * 8 + u
            at = pl.multiple_of(i * PITCH, PITCH)
            a_re = wre[pl.ds(at, PITCH), :]
            a_im = wim[pl.ds(at, PITCH), :]
            for j in range(TOP):
                t = pl.multiple_of(idx[i * TOP + j] * PITCH, PITCH)
                b_re = rre[pl.ds(t, PITCH), :]
                b_im = rim[pl.ds(t, PITCH), :]
                p = a_re * b_re + a_im * b_im
                q = a_im * b_re - a_re * b_im
                rows[j][0].append(jnp.sum(p, axis=0, keepdims=True))
                rows[j][1].append(jnp.sum(q, axis=0, keepdims=True))
        at = pl.multiple_of(b * 8, 8)
        for j in range(TOP):
            pq[j, pl.ds(at, 8), :LANES] = jnp.concatenate(rows[j][0], axis=0)
            pq[j, pl.ds(at, 8), LANES:] = jnp.concatenate(rows[j][1], axis=0)
        return carry

    lax.fori_loop(0, PARTICLES // 8, block, 0)
    logits = [dot_exact(pq[j], logit[...])[:, :NA] for j in range(TOP)]
    logits.append(jnp.zeros((PARTICLES, LOGIT_W - TOP * NA), f32))
    out[...] = jnp.concatenate(logits, axis=1)


def softmax_kernel(parts, out):
    logits = parts[0]
    for k in range(1, MEMBERS):
        logits += parts[k]
    lane = lax.broadcasted_iota(jnp.int32, logits.shape, 1)
    logits = jnp.where(lane < TOP * NA, logits, -jnp.inf)
    highest = jnp.max(logits, axis=1, keepdims=True)
    e = jnp.exp(logits - highest)
    posterior = (e / jnp.sum(e, axis=1, keepdims=True)).astype(bf16)
    for k in range(MEMBERS):
        out[k] = posterior


def gather_kernel(idx, post, both, inverse, wre, wim, out, gre, gim, are, aim, total):
    for j in range(TOP):
        x = lanes_of(post, j // 2)
        y = sum(dot(x, window(both, (j % 2, k), j // 2)) for k in range(2))
        gre[j] = y[:, :LANES]
        gim[j] = y[:, LANES:]
    are[...] = jnp.zeros_like(are)
    aim[...] = jnp.zeros_like(aim)

    def block(b, carry):
        for u in range(4):
            i = b * 4 + u
            at = pl.multiple_of(i * PITCH, PITCH)
            a_re = wre[pl.ds(at, PITCH), :]
            a_im = wim[pl.ds(at, PITCH), :]
            places, sums = [], []
            for j in range(TOP):
                t = pl.multiple_of(idx[i * TOP + j] * PITCH, PITCH)
                g_re = gre[j, pl.ds(i, 1), :]
                g_im = gim[j, pl.ds(i, 1), :]
                places.append(t)
                sums.append(
                    (
                        are[pl.ds(t, PITCH), :] + (a_re * g_re + a_im * g_im),
                        aim[pl.ds(t, PITCH), :] + (a_im * g_re - a_re * g_im),
                    )
                )
            for j in range(TOP):
                are[pl.ds(places[j], PITCH), :] = sums[j][0]
                aim[pl.ds(places[j], PITCH), :] = sums[j][1]
        return carry

    lax.fori_loop(0, PARTICLES // 4, block, 0)
    total[...] = jnp.zeros_like(total)
    for s in range(WINDOWS):
        x = jnp.concatenate(
            [
                are[pl.ds(s, TABLE_ROWS, stride=PITCH), :],
                aim[pl.ds(s, TABLE_ROWS, stride=PITCH), :],
            ],
            axis=1,
        )
        hi = x.astype(bf16)
        low = (x - hi.astype(f32)).astype(bf16)
        t_hi, t_low = window(inverse, (0,), s), window(inverse, (1,), s)
        total[:, LANES * s : LANES * s + 2 * LANES] += (
            dot_t(hi, t_hi) + dot_t(low, t_hi) + dot_t(hi, t_low)
        )
    out[...] = total[...].reshape(OWNERS, 8, SEND_W).astype(bf16)


def final_kernel(parts, below, out):
    sums = []
    for h in range(2):
        members = [s for s in range(OWNERS) if (s // 8) % 2 == h]
        total = parts[members[0]].astype(f32)
        for s in members[1:]:
            total += parts[s].astype(f32)
        sums.append(total)
    total = jnp.concatenate(sums, axis=0)
    under = dot_exact(total[:, 512:] + 1.0, below[...].astype(f32))[:, :IMG_W]
    new = total[:, :IMG_W] / under
    out[:, :IMG_W] = new[:7]
    out[:, IMG_W:] = new[8:15]


VM = pl.BlockSpec(memory_space=pltpu.VMEM)
SM = pl.BlockSpec(memory_space=pltpu.SMEM)
PARAMS = pltpu.CompilerParams(vmem_limit_bytes=24 * 1024 * 1024)


def call(kernel, name, out_shape, in_specs, args, scratch=()):
    out_specs = tuple(VM for _ in out_shape) if isinstance(out_shape, tuple) else VM
    return pl.pallas_call(
        kernel,
        out_shape=out_shape,
        in_specs=in_specs,
        out_specs=out_specs,
        scratch_shapes=scratch,
        compiler_params=PARAMS,
        name=name,
    )(*args)


def on_device(images, ctf, classes, class_place, references, sigma2):
    fwd, side, inverse, both, logit, spread, below = make_tables()
    img, h = lax.axis_index("img"), lax.axis_index("xl")
    shape = jax.ShapeDtypeStruct
    wsend, rsend = call(
        pack_kernel,
        "pack",
        (shape((MEMBERS, 16, SEND_W), bf16), shape((OWNERS, 8, REF_W), bf16)),
        [SM] + [VM] * 5,
        (img.reshape(1), images, ctf, classes, class_place.reshape(1, -1), references),
    )
    wrecv = lax.all_to_all(wsend, GROUP, 0, 0, tiled=True).reshape(PARTICLES, SEND_W)
    rrecv = lax.all_to_all(rsend, CLS, 0, 0, tiled=True)
    table_rows = wrecv[:, ROW_W : ROW_W + TOP].astype(jnp.int32)
    idx = (table_rows // 7 * 8 + table_rows % 7).reshape(-1)
    inv = 1.0 / lax.dynamic_slice(sigma2, (img * 8 + h * SHELLS,), (SHELLS,))
    inv = jnp.concatenate(
        [jnp.repeat(inv, PAIR), jnp.repeat(inv, NA), jnp.zeros((SEND_W - ROW_W,), f32)]
    ).reshape(1, SEND_W)
    hat = shape((PARTICLES * PITCH, LANES), f32)
    wre, wim = call(weigh_kernel, "weigh", (hat, hat), [VM] * 4, (wrecv, inv, spread, fwd))
    table = pltpu.VMEM((TABLE_ROWS * PITCH, LANES), f32)
    partial = call(
        score_kernel,
        "score",
        shape((PARTICLES, LOGIT_W), f32),
        [SM] + [VM] * 6,
        (idx, rrecv, fwd, side, logit, wre, wim),
        [table, table, pltpu.VMEM((TOP, PARTICLES, 2 * LANES), f32)],
    )
    parts = lax.all_to_all(partial.reshape(MEMBERS, 16, LOGIT_W), GROUP, 0, 0, tiled=True)
    post = call(
        softmax_kernel, "softmax", shape((MEMBERS, 16, LOGIT_W), bf16), [VM], (parts,)
    )
    post = lax.all_to_all(post, GROUP, 0, 0, tiled=True).reshape(PARTICLES, LOGIT_W)
    each = pltpu.VMEM((TOP, PARTICLES, LANES), f32)
    sums = call(
        gather_kernel,
        "gather",
        shape((OWNERS, 8, SEND_W), bf16),
        [SM] + [VM] * 5,
        (idx, post, both, inverse, wre, wim),
        [each, each, table, table, pltpu.VMEM((TABLE_ROWS, SEND_W), f32)],
    )
    arrived = lax.all_to_all(sums, CLS, 0, 0, tiled=True)
    return call(
        final_kernel, "final", shape((7, 2 * IMG_W), f32), [VM, VM], (arrived, below)
    )


def solution(mesh):
    finer = Mesh(mesh.devices.reshape(2, 2, 8, 8), DEVICES)
    in_specs = (
        P(DEVICES, None),
        P(DEVICES, None),
        P(DEVICES, None),
        P(),
        P(CLS, None),
        P(),
    )
    return jax.shard_map(
        on_device, mesh=finer, in_specs=in_specs, out_specs=P(CLS, "img"), check_vma=False
    )
```

time: 122 us -> 103 us (0.84)
  Pallas kernels: 27.4 us -> 13.8 us
  blocking collectives: 66.5 us -> 59.6 us
  local copies, waits for them, and re-layouts: 3.78 us -> 7.96 us
  waiting for transfers between devices: 12.3 us -> 10 us
    pallas_call x6, Pallas kernels: 27.4 us -> 13.8 us  [call(): pl.pallas_call(kernel, out_shape=out_shape, in_specs=in_specs, out_specs=...]
    all_to_all x4, blocking collectives: 66.5 us -> 59.6 us  [the longest x1 21.4 us: on_device(): arrived = lax.all_to_all(sums, CLS, 0, 0, tiled=True)]
    unnamed x7 -> x25, local copies, waits for them, and re-layouts: 2.19 us -> 7.53 us
    all_to_all x1, waiting for transfers between devices: 12.3 us -> 10 us  [on_device(): rrecv = lax.all_to_all(rsend, CLS, 0, 0, tiled=True)]
  transfers between devices with their start and end apart: 1 -> 1, of which waited for: 1 -> 1; matrix products, arithmetic and copies ran while one was open for 2% -> 1% of each run, Pallas kernels for 4% -> 1%
where the time goes in v2:
time: 103 us
  blocking collectives  59.6 us (58%)
  Pallas kernels  13.8 us (13%)
  starting transfers between devices  10.9 us (11%)
  waiting for transfers between devices  10 us (10%)
  local copies, waits for them, and re-layouts  7.96 us (8%)
    all_to_all x1, blocking collectives, on_device(): arrived = lax.all_to_all(sums, CLS, 0, 0, tiled=True)  21.4 us
    all_to_all x1, blocking collectives, on_device(): lax.all_to_all(wsend, GROUP, 0, 0, tiled=True).reshape(PARTICLES, SEND_W)  15.4 us
    pallas_call x6, Pallas kernels, call(): pl.pallas_call(kernel, out_shape=out_shape, in_specs=in_specs, out_specs=...  13.8 us
    all_to_all x1, blocking collectives, on_device(): lax.all_to_all(partial.reshape(MEMBERS, 16, LOGIT_W), GROUP, 0, 0, tiled=...  12.8 us
    all_to_all x1, starting transfers between devices, on_device(): rrecv = lax.all_to_all(rsend, CLS, 0, 0, tiled=True)  10.9 us
    all_to_all x1, waiting for transfers between devices, on_device(): rrecv = lax.all_to_all(rsend, CLS, 0, 0, tiled=True)  10 us
    all_to_all x1, blocking collectives, on_device(): lax.all_to_all(post, GROUP, 0, 0, tiled=True).reshape(PARTICLES, LOGIT_W)  9.97 us
    unnamed x25, local copies, waits for them, and re-layouts  7.53 us
  transfers between devices with their start and end apart: 1, of which 1 were waited for; matrix products, arithmetic and copies ran while one was open for 1% of the time, Pallas kernels for 1%

profile of v2, /device:TPU:32, one launch (start us, length us, event | category | flops | bytes accessed | tf_op | source)
XLA Modules:
  0.0 102.7 jit_solution(5351277664082400381)
XLA Ops:
  0.0 0.8 copy.15.classes
  0.8 1.0 copy-done.6
  1.7 0.9 copy-done.7
  2.6 0.9 copy-done.8
  3.6 0.7 copy-done.10
  4.2 1.1 %pack.1 = (bf16[16,16,896]{2,1,0:T(8,128)(2,1)S(1)}, bf16[32,8,640]{2,1,0:T(8,128)(2,1)}) custom-call(s32[1]{0:T(128)} %bitcast.at_ref, bf16[16,9216]{1,0:T(8,128)(2,1)S(1)} %copy-done.6, bf16[16,4608]{1,0:T(8,128)(2,1)S(1)} %copy-done.7, s32[16,4]{1,0:T(8,128)S(1)} %copy.15.classes, s32[1,224]{1,0:T(1,128)S(1)} %bitcast.9, bf16[7,9216]{1,0:T(8,128)(2,1)S(1)} %copy-done.8), custom_call_target="tpu_custom_call" | custom-call | tf_op jit(solution)/shard_map/pack/pallas_call | solution.py:293
  5.3 15.4 %all_to_all.25 = bf16[16,16,896]{2,1,0:T(8,128)(2,1)S(1)} all-to-all(bf16[16,16,896]{2,1,0:T(8,128)(2,1)S(1)} %get-tuple-element.9), channel_id=1, replica_groups=mesh['xh'=2,'xl'=2,'z'=8,'img'=8] {'xl','img'}, dimensions={0} | all-to-all | bytes 917504 | tf_op jit(solution)/shard_map/all_to_all | solution.py:315
  20.7 10.9 %all-to-all-start.1 = ((bf16[32,8,640]{2,1,0:T(8,128)(2,1)}), bf16[32,8,640]{2,1,0:T(8,128)(2,1)S(1)}, u32[]{:S(2)}, u32[]{:S(2)}) async-start(bf16[32,8,640]{2,1,0:T(8,128)(2,1)} %get-tuple-element.10), calls=%async_computation.1 | async-start | bytes 655360 | tf_op jit(solution)/shard_map/all_to_all | solution.py:316
  31.7 0.1 dynamic-slice_divide_fusion
  31.7 0.1 broadcast_in_dim.10
  31.8 0.1 reshape.32
  31.9 0.1 broadcast_in_dim.9
  32.0 0.1 reshape.31
  32.1 0.1 pad_maximum_fusion
  32.1 0.2 fusion.4
  32.4 0.1 reshape.30.idx
  32.5 0.0 copy-start.3
  32.5 1.1 %copy-done.3 = bf16[384,896]{1,0:T(8,128)(2,1)S(1)} copy-done((bf16[384,896]{1,0:T(8,128)(2,1)S(1)}, bf16[384,896]{1,0:T(8,128)(2,1)}, u32[]{:S(2)}) %copy-start.3) | copy-done | bytes 688152
  33.6 1.1 %weigh.1 = (f32[2048,128]{1,0:T(8,128)S(1)}, f32[2048,128]{1,0:T(8,128)S(1)}) custom-call(bf16[256,896]{1,0:T(8,128)(2,1)S(1)} %bitcast.6, f32[1,896]{1,0:T(1,128)S(1)} %reshape.33.inv, bf16[384,896]{1,0:T(8,128)(2,1)S(1)} %copy-done.3, bf16[3,384,256]{2,1,0:T(8,128)(2,1)S(1)} %copy-done), custom_call_target="tpu_custom_call" | custom-call | tf_op jit(solution)/shard_map/weigh/pallas_call | solution.py:293
  34.7 10.0 %all-to-all-done.1.recv = bf16[32,8,640]{2,1,0:T(8,128)(2,1)S(1)} async-done(((bf16[32,8,640]{2,1,0:T(8,128)(2,1)}), bf16[32,8,640]{2,1,0:T(8,128)(2,1)S(1)}, u32[]{:S(2)}, u32[]{:S(2)}) %all-to-all-start.1) | async-done | bytes 327712 | tf_op jit(solution)/shard_map/all_to_all | solution.py:316
  44.7 1.3 %copy-done.1 = bf16[2,3,384,256]{3,2,1,0:T(8,128)(2,1)S(1)} copy-done((bf16[2,3,384,256]{3,2,1,0:T(8,128)(2,1)S(1)}, bf16[2,3,384,256]{3,2,1,0:T(8,128)(2,1)}, u32[]{:S(2)}) %copy-start.1) | copy-done | bytes 1179672
  46.0 0.9 copy-done.9
  46.9 5.8 %score.1 = f32[256,384]{1,0:T(8,128)S(1)} custom-call(s32[1024]{0:T(1024)S(1)} %reshape.30.idx, bf16[32,8,640]{2,1,0:T(8,128)(2,1)S(1)} %all-to-all-done.1.recv, bf16[3,384,256]{2,1,0:T(8,128)(2,1)S(1)} %copy-done, bf16[2,3,384,256]{3,2,1,0:T(8,128)(2,1)S(1)} %copy-done.1, f32[256,128]{1,0:T(8,128)S(1)} %copy-done.9, f32[2048,128]{1,0:T(8,128)S(1)} %get-tuple-element.11.wre, ...), custom_call_target="tpu_custom_call" | custom-call | tf_op jit(solution)/shard_map/score/pallas_call | solution.py:293
  52.8 0.0 copy-start.2
  52.8 0.0 copy-start.5
  52.8 12.8 %all_to_all.26.parts = f32[16,16,384]{2,1,0:T(8,128)S(1)} all-to-all(f32[16,16,384]{2,1,0:T(8,128)S(1)} %bitcast.7), channel_id=1, replica_groups=mesh['xh'=2,'xl'=2,'z'=8,'img'=8] {'xl','img'}, dimensions={0} | all-to-all | bytes 786432 | tf_op jit(solution)/shard_map/all_to_all | solution.py:334
  65.5 0.2 softmax.1
  65.8 10.0 %all_to_all.27 = bf16[16,16,384]{2,1,0:T(8,128)(2,1)S(1)} all-to-all(bf16[16,16,384]{2,1,0:T(8,128)(2,1)S(1)} %softmax.1), channel_id=1, replica_groups=mesh['xh'=2,'xl'=2,'z'=8,'img'=8] {'xl','img'}, dimensions={0} | all-to-all | bytes 393216 | tf_op jit(solution)/shard_map/all_to_all | solution.py:338
  75.7 4.3 %gather.1 = bf16[32,8,896]{2,1,0:T(8,128)(2,1)S(1)} custom-call(s32[1024]{0:T(1024)S(1)} %reshape.30.idx, bf16[256,384]{1,0:T(8,128)(2,1)S(1)} %bitcast.8, bf16[2,2,384,256]{3,2,1,0:T(8,128)(2,1)S(1)} %copy-done.2, bf16[2,384,256]{2,1,0:T(8,128)(2,1)S(1)} %copy-done.5, f32[2048,128]{1,0:T(8,128)S(1)} %get-tuple-element.11.wre, ...), custom_call_target="tpu_custom_call" | custom-call | tf_op jit(solution)/shard_map/gather/pallas_call | solution.py:293
  80.1 0.0 copy-start.4
  80.1 21.4 %all_to_all.28.parts = bf16[32,8,896]{2,1,0:T(8,128)(2,1)S(1)} all-to-all(bf16[32,8,896]{2,1,0:T(8,128)(2,1)S(1)} %gather.1), channel_id=1, replica_groups=mesh['xh'=2,'xl'=2,'z'=8,'img'=8] {'xh','xl','z'}, dimensions={0} | all-to-all | bytes 917504 | tf_op jit(solution)/shard_map/all_to_all | solution.py:348
  101.5 1.3 %final.1 = f32[7,1152]{1,0:T(8,128)} custom-call(bf16[32,8,896]{2,1,0:T(8,128)(2,1)S(1)} %all_to_all.28.parts, bf16[384,640]{1,0:T(8,128)(2,1)S(1)} %copy-done.4), custom_call_target="tpu_custom_call" | custom-call | tf_op jit(solution)/shard_map/final/pallas_call | solution.py:293
  (15 shorter events, 0.0 us)
Async XLA Ops:
  0.0 31.7 %copy-start.11 = (f32[64]{0:T(128)S(1)}, f32[64]{0:T(128)}, u32[]{:S(2)}) copy-start(f32[64]{0:T(128)} %param.18) | copy-start | bytes 772
  0.8 1.0 copy-start.6
  1.7 0.9 copy-start.7
  2.6 0.9 copy-start.8
  3.6 0.7 copy-start.10
  4.2 28.3 %copy-start = (bf16[3,384,256]{2,1,0:T(8,128)(2,1)S(1)}, bf16[3,384,256]{2,1,0:T(8,128)(2,1)}, u32[]{:S(2)}) copy-start(bf16[3,384,256]{2,1,0:T(8,128)(2,1)} %constant.57.clone.fwd) | copy-start | bytes 1769476
  20.7 24.0 %all-to-all-start.1 = ((bf16[32,8,640]{2,1,0:T(8,128)(2,1)}), bf16[32,8,640]{2,1,0:T(8,128)(2,1)S(1)}, u32[]{:S(2)}, u32[]{:S(2)}) async-start(bf16[32,8,640]{2,1,0:T(8,128)(2,1)} %get-tuple-element.10), calls=%async_computation.1 | async-start | bytes 655360 | tf_op jit(solution)/shard_map/all_to_all | solution.py:316
  32.5 1.1 %copy-start.3 = (bf16[384,896]{1,0:T(8,128)(2,1)S(1)}, bf16[384,896]{1,0:T(8,128)(2,1)}, u32[]{:S(2)}) copy-start(bf16[384,896]{1,0:T(8,128)(2,1)} %constant.56.clone.spread) | copy-start | bytes 2064388
  44.7 1.3 %copy-start.1 = (bf16[2,3,384,256]{3,2,1,0:T(8,128)(2,1)S(1)}, bf16[2,3,384,256]{3,2,1,0:T(8,128)(2,1)}, u32[]{:S(2)}) copy-start(bf16[2,3,384,256]{3,2,1,0:T(8,128)(2,1)} %constant.58.clone.side) | copy-start | bytes 3538948
  46.0 0.9 copy-start.9
  52.8 23.0 %copy-start.2 = (bf16[2,2,384,256]{3,2,1,0:T(8,128)(2,1)S(1)}, bf16[2,2,384,256]{3,2,1,0:T(8,128)(2,1)}, u32[]{:S(2)}) copy-start(bf16[2,2,384,256]{3,2,1,0:T(8,128)(2,1)} %constant.60.clone.both) | copy-start | bytes 2359300
  52.8 23.0 %copy-start.5 = (bf16[2,384,256]{2,1,0:T(8,128)(2,1)S(1)}, bf16[2,384,256]{2,1,0:T(8,128)(2,1)}, u32[]{:S(2)}) copy-start(bf16[2,384,256]{2,1,0:T(8,128)(2,1)} %constant.61.clone.inverse) | copy-start | bytes 1179652
  80.1 21.4 %copy-start.4 = (bf16[384,640]{1,0:T(8,128)(2,1)S(1)}, bf16[384,640]{1,0:T(8,128)(2,1)}, u32[]{:S(2)}) copy-start(bf16[384,640]{1,0:T(8,128)(2,1)} %constant.62.clone.below) | copy-start | bytes 1474564

commit v3 on v2

v3 whole, which is shorter than its diff:
```python
import jax
import jax.numpy as jnp
import numpy as np
from jax import lax
from jax.experimental import pallas as pl
from jax.experimental.pallas import tpu as pltpu
from jax.sharding import Mesh
from jax.sharding import PartitionSpec as P

TOP = 4
NA = 72
HALF = 64
LANES = 128
PITCH = 8
SHELLS = 4
WINDOWS = 6
MEMBERS = 16
PARTICLES = 16 * MEMBERS
OWNERS = 32
TABLE_ROWS = 8 * OWNERS
PAIR = 2 * NA
IMG_W = SHELLS * PAIR
CTF_W = SHELLS * NA
REF_W = 640
ROW_W = IMG_W + CTF_W
SEND_W = 896
LOGIT_W = 384
FREQS = NA // 2 + 1
TOPPAD = 112
TABLE = 384
CLS = ("xh", "xl", "z")
GROUP = ("xl", "img")
DEVICES = ("xh", "xl", "z", "img")

bf16 = jnp.bfloat16
f32 = jnp.float32


def split3(x):
    x = np.asarray(x, np.float32)
    hi = x.astype(bf16)
    rest = x - hi.astype(np.float32)
    mid = rest.astype(bf16)
    low = (rest - mid.astype(np.float32)).astype(bf16)
    return np.stack([hi, mid, low])


def make_tables():
    freq = np.arange(FREQS)
    angle = np.arange(NA)
    phase = (freq[None, :] * angle[:, None]) % NA * (2.0 * np.pi / NA)
    cos, sin = np.cos(phase), np.sin(phase)
    forward = np.zeros((TABLE, 2 * LANES))
    for part in range(2):
        rows = slice(TOPPAD + part * NA, TOPPAD + part * NA + NA)
        re = slice(part * HALF, part * HALF + FREQS)
        im = slice(LANES + part * HALF, LANES + part * HALF + FREQS)
        forward[rows, re], forward[rows, im] = cos, -sin
    lane = np.arange(SEND_W)
    source = np.where(lane < IMG_W, IMG_W + NA * (lane // PAIR) + lane % NA, lane) - 512
    spread = (np.arange(384)[:, None] == source[None, :]) & (lane < ROW_W)[None, :]
    return split3(forward), spread.astype(bf16)


def dot(a, b):
    return lax.dot_general(a, b, (((1,), (0,)), ((), ())), preferred_element_type=f32)


def dot_t(a, b):
    return lax.dot_general(a, b, (((1,), (1,)), ((), ())), preferred_element_type=f32)


def dot_exact(a, b):
    return lax.dot_general(
        a,
        b,
        (((1,), (0,)), ((), ())),
        precision=lax.Precision.HIGHEST,
        preferred_element_type=f32,
    )


def window(table, block, index):
    start = TOPPAD - 16 * index
    return table[block, start : start + 2 * LANES, :]


def lanes_of(x, index):
    return x[:, LANES * index : LANES * index + 2 * LANES]


def lane_index(shape):
    return lax.broadcasted_iota(jnp.int32, shape, len(shape) - 1)


def inverse_weights():
    freq = lane_index((1, LANES)) % HALF
    ends = (freq == 0) | (freq == NA // 2)
    return jnp.where(freq < FREQS, jnp.where(ends, 1.0 / NA, 2.0 / NA), 0.0).astype(f32)


def rows_summed(tiles):
    line = lax.broadcasted_iota(jnp.int32, (8, LANES), 0)
    for k in (1, 2, 4):
        mine = (line & k) == 0
        tiles = [
            jnp.where(mine, a, b) + pltpu.roll(jnp.where(mine, b, a), 8 - k, 0)
            for a, b in zip(tiles[::2], tiles[1::2])
        ]
    return tiles[0]


def forward_wave(x, table, index, splits=3):
    return sum(dot(x, window(table, k, index)) for k in range(splits))


def pack_kernel(images, ctf, classes, place, wsend):
    width = SEND_W - ROW_W
    lookup = place[...].astype(f32).astype(bf16)
    line = lax.broadcasted_iota(jnp.int32, (16, 16), 0)
    listed = jnp.zeros((16, 16), f32)
    for j in range(TOP):
        hit = classes[j : j + 1, :] == lax.broadcasted_iota(jnp.int32, (place.shape[1], 16), 0)
        row = dot(lookup, jnp.where(hit, 1.0, 0.0).astype(bf16))
        listed = jnp.where(line == j, row, listed)
    tail = jnp.concatenate([listed, jnp.zeros((16, width - 16), f32)], axis=1).astype(bf16)
    for h in range(2):
        for i in range(8):
            shell = i * 8 + h * SHELLS
            wsend[h * 8 + i] = jnp.concatenate(
                [
                    images[:, shell * PAIR : shell * PAIR + IMG_W],
                    ctf[:, shell * NA : shell * NA + CTF_W],
                    tail,
                ],
                axis=1,
            )


def copies_kernel(at, refs, rsend):
    start = pl.multiple_of(at[0] * 2 * IMG_W, LANES)
    mine = refs[:, pl.ds(start, 2 * IMG_W)].astype(f32)
    for h in range(2):
        half = mine[:, h * IMG_W : (h + 1) * IMG_W]
        half = jnp.concatenate([half, jnp.zeros((7, REF_W - IMG_W), f32)], axis=1)
        half = jnp.concatenate([half, jnp.zeros((1, REF_W), f32)], axis=0).astype(bf16)
        for o in range(OWNERS):
            if (o // 8) % 2 == h:
                rsend[o] = half


def weigh_kernel(recv, inv, spread, table, wre, wim):
    scale = dot(recv[:, 512:], spread[...]) * inv[...]
    weighted = (recv[...].astype(f32) * scale).astype(bf16)
    for s in range(WINDOWS):
        y = forward_wave(lanes_of(weighted, s), table, s)
        wre[pl.ds(s, PARTICLES, stride=PITCH), :] = y[:, :LANES]
        wim[pl.ds(s, PARTICLES, stride=PITCH), :] = y[:, LANES:]
    zero = jnp.zeros((PARTICLES, LANES), f32)
    for s in range(WINDOWS, PITCH):
        wre[pl.ds(s, PARTICLES, stride=PITCH), :] = zero
        wim[pl.ds(s, PARTICLES, stride=PITCH), :] = zero


def score_kernel(idx, recv, table, wre, wim, out, rre, rim, pq):
    raw32 = recv[...].astype(f32).reshape(TABLE_ROWS, REF_W)
    raw = raw32.astype(bf16)
    square = raw32 * raw32
    left = square + jnp.concatenate([square[:, NA:], square[:, :NA]], axis=1)
    right = square + jnp.concatenate([square[:, REF_W - NA :], square[:, : REF_W - NA]], axis=1)
    lane = lane_index((1, REF_W))
    even = (lane < NA) | ((lane >= 2 * PAIR) & (lane < 2 * PAIR + NA))
    odd = ((lane >= PAIR + NA) & (lane < 2 * PAIR)) | (
        (lane >= 3 * PAIR + NA) & (lane < 4 * PAIR)
    )
    power = jnp.where(even, left, jnp.where(odd, right, 0.0)).astype(bf16).astype(f32)
    power = (-0.5 * power).astype(bf16)
    for s in range(SHELLS):
        y = forward_wave(lanes_of(raw, s), table, s)
        rre[pl.ds(s, TABLE_ROWS, stride=PITCH), :] = y[:, :LANES]
        rim[pl.ds(s, TABLE_ROWS, stride=PITCH), :] = y[:, LANES:]
    for j in range(SHELLS // 2):
        y = sum(forward_wave(lanes_of(power, s), table, s) for s in (2 * j, 2 * j + 1))
        rre[pl.ds(SHELLS + j, TABLE_ROWS, stride=PITCH), :] = y[:, :LANES]
        rim[pl.ds(SHELLS + j, TABLE_ROWS, stride=PITCH), :] = y[:, LANES:]
    zero = jnp.zeros((TABLE_ROWS, LANES), f32)
    for s in range(WINDOWS, PITCH):
        rre[pl.ds(s, TABLE_ROWS, stride=PITCH), :] = zero
        rim[pl.ds(s, TABLE_ROWS, stride=PITCH), :] = zero

    def block(b, carry):
        rows = [[[], []] for _ in range(TOP)]
        for u in range(8):
            i = b * 8 + u
            at = pl.multiple_of(i * PITCH, PITCH)
            a_re = wre[pl.ds(at, PITCH), :]
            a_im = wim[pl.ds(at, PITCH), :]
            for j in range(TOP):
                t = pl.multiple_of(idx[b // 2 * 64 + j * 16 + b % 2 * 8 + u] * PITCH, PITCH)
                b_re = rre[pl.ds(t, PITCH), :]
                b_im = rim[pl.ds(t, PITCH), :]
                p = a_re * b_re + a_im * b_im
                q = a_im * b_re - a_re * b_im
                rows[j][0].append(p)
                rows[j][1].append(q)
        at = pl.multiple_of(b * 8, 8)
        for j in range(TOP):
            pq[j, pl.ds(at, 8), :LANES] = rows_summed(rows[j][0])
            pq[j, pl.ds(at, 8), LANES:] = rows_summed(rows[j][1])
        return carry

    lax.fori_loop(0, PARTICLES // 8, block, 0)
    weights = inverse_weights()
    low = lane_index((1, LANES)) < HALF
    windows = []
    for j in range(0, TOP, 2):
        sides = []
        for at in (0, LANES):
            first, second = pq[j, :, at : at + LANES], pq[j + 1, :, at : at + LANES]
            first = first + pltpu.roll(first, HALF, 1)
            second = second + pltpu.roll(second, HALF, 1)
            sides.append(jnp.where(low, first, second) * weights)
        x = jnp.concatenate(sides, axis=1)
        hi = x.astype(bf16)
        rest = x - hi.astype(f32)
        mid = rest.astype(bf16)
        small = (rest - mid.astype(f32)).astype(bf16)
        t = [window(table, k, j // 2) for k in range(3)]
        y = dot_t(small, t[0]) + dot_t(hi, t[2]) + dot_t(mid, t[1])
        y = y + (dot_t(mid, t[0]) + dot_t(hi, t[1]))
        windows.append(y + dot_t(hi, t[0]))
    out[:, :LANES] = windows[0][:, :LANES]
    out[:, LANES : 2 * LANES] = windows[0][:, LANES:] + windows[1][:, :LANES]
    out[:, 2 * LANES :] = windows[1][:, LANES:]


def softmax_kernel(parts, out):
    logits = parts[0]
    for k in range(1, MEMBERS):
        logits += parts[k]
    logits = jnp.where(lane_index(logits.shape) < TOP * NA, logits, -jnp.inf)
    highest = jnp.max(logits, axis=1, keepdims=True)
    e = jnp.exp(logits - highest)
    posterior = (e / jnp.sum(e, axis=1, keepdims=True)).astype(bf16)
    for k in range(MEMBERS):
        out[k] = posterior


def gather_kernel(idx, post, table, wre, wim, out, gre, gim, are, aim):
    lane = lane_index((1, 2 * LANES))
    for j in range(TOP):
        first = 16 * (j // 2) + NA * (j % 2)
        mine = (lane >= first) & (lane < first + NA)
        x = jnp.where(mine, lanes_of(post[...].astype(f32), j // 2), 0.0).astype(bf16)
        y = forward_wave(x, table, j // 2, splits=2)
        gre[j] = y[:, :LANES] + pltpu.roll(y[:, :LANES], HALF, 1)
        gim[j] = y[:, LANES:] + pltpu.roll(y[:, LANES:], HALF, 1)
    are[...] = jnp.zeros_like(are)
    aim[...] = jnp.zeros_like(aim)

    def block(b, carry):
        for u in range(4):
            i = b * 4 + u
            at = pl.multiple_of(i * PITCH, PITCH)
            a_re = wre[pl.ds(at, PITCH), :]
            a_im = wim[pl.ds(at, PITCH), :]
            pending = []
            for j in range(TOP):
                where = b // 4 * 64 + j * 16 + b % 4 * 4 + u
                t = pl.multiple_of(idx[where] * PITCH, PITCH)
                g_re = gre[j, pl.ds(i, 1), :]
                g_im = gim[j, pl.ds(i, 1), :]
                pending.append((are, t, are[pl.ds(t, PITCH), :] + (a_re * g_re + a_im * g_im)))
                pending.append((aim, t, aim[pl.ds(t, PITCH), :] + (a_im * g_re - a_re * g_im)))
            for ref, t, value in pending:
                ref[pl.ds(t, PITCH), :] = value
        return carry

    lax.fori_loop(0, PARTICLES // 4, block, 0)
    weights = inverse_weights()
    before = None
    for s in range(WINDOWS):
        lines = pl.ds(s, TABLE_ROWS, stride=PITCH)
        x = jnp.concatenate(
            [are[lines, :] * weights, aim[lines, :] * weights], axis=1
        )
        hi = x.astype(bf16)
        low = (x - hi.astype(f32)).astype(bf16)
        t_hi, t_low = window(table, 0, s), window(table, 1, s)
        y = dot_t(hi, t_hi) + dot_t(low, t_hi) + dot_t(hi, t_low)
        tile = y[:, :LANES] if before is None else before + y[:, :LANES]
        out[:, :, LANES * s : LANES * s + LANES] = tile.reshape(OWNERS, 8, LANES).astype(bf16)
        before = y[:, LANES:]
    out[:, :, LANES * WINDOWS :] = before.reshape(OWNERS, 8, LANES).astype(bf16)


def final_kernel(parts, spread, out):
    sums = []
    for h in range(2):
        members = [s for s in range(OWNERS) if (s // 8) % 2 == h]
        total = parts[members[0]].astype(f32)
        for s in members[1:]:
            total += parts[s].astype(f32)
        sums.append(total)
    total = jnp.concatenate(sums, axis=0)
    under = dot_exact(total[:, 512:] + 1.0, spread[:, :REF_W].astype(f32))[:, :IMG_W]
    new = total[:, :IMG_W] / under
    out[:, :IMG_W] = new[:7]
    out[:, IMG_W:] = new[8:15]


VM = pl.BlockSpec(memory_space=pltpu.VMEM)
SM = pl.BlockSpec(memory_space=pltpu.SMEM)


def call(kernel, name, out_shape, in_specs, args, scratch=(), limit=24):
    out_specs = tuple(VM for _ in out_shape) if isinstance(out_shape, tuple) else VM
    return pl.pallas_call(
        kernel,
        out_shape=out_shape,
        in_specs=in_specs,
        out_specs=out_specs,
        scratch_shapes=scratch,
        compiler_params=pltpu.CompilerParams(vmem_limit_bytes=limit * 1024 * 1024),
        name=name,
    )(*args)


def on_device(images, ctf, classes, class_place, references, sigma2):
    table, spread = make_tables()
    img, h = lax.axis_index("img"), lax.axis_index("xl")
    shape = jax.ShapeDtypeStruct
    wsend = call(
        pack_kernel,
        "pack",
        shape((MEMBERS, 16, SEND_W), bf16),
        [VM] * 4,
        (images, ctf, classes.T, class_place.reshape(1, -1)),
        limit=58,
    )
    rsend = call(
        copies_kernel,
        "copies",
        shape((OWNERS, 8, REF_W), bf16),
        [SM, VM],
        (img.reshape(1), references),
        limit=8,
    )
    wrecv = lax.all_to_all(wsend, GROUP, 0, 0, tiled=True)
    rrecv = lax.all_to_all(rsend, CLS, 0, 0, tiled=True)
    listed = wrecv[:, :TOP, ROW_W : ROW_W + 16].astype(jnp.int32)
    idx = (listed // 7 * 8 + listed % 7).reshape(-1)
    wrecv = wrecv.reshape(PARTICLES, SEND_W)
    inv = 1.0 / lax.dynamic_slice(sigma2, (img * 8 + h * SHELLS,), (SHELLS,))
    inv = jnp.concatenate(
        [jnp.repeat(inv, PAIR), jnp.repeat(inv, NA), jnp.zeros((SEND_W - ROW_W,), f32)]
    ).reshape(1, SEND_W)
    hat = shape((PARTICLES * PITCH, LANES), f32)
    wre, wim = call(
        weigh_kernel, "weigh", (hat, hat), [VM] * 4, (wrecv, inv, spread, table)
    )
    rows = pltpu.VMEM((TABLE_ROWS * PITCH, LANES), f32)
    partial = call(
        score_kernel,
        "score",
        shape((PARTICLES, LOGIT_W), f32),
        [SM] + [VM] * 4,
        (idx, rrecv, table, wre, wim),
        [rows, rows, pltpu.VMEM((TOP, PARTICLES, 2 * LANES), f32)],
    )
    parts = lax.all_to_all(partial.reshape(MEMBERS, 16, LOGIT_W), GROUP, 0, 0, tiled=True)
    post = call(
        softmax_kernel, "softmax", shape((MEMBERS, 16, LOGIT_W), bf16), [VM], (parts,)
    )
    post = lax.all_to_all(post, GROUP, 0, 0, tiled=True).reshape(PARTICLES, LOGIT_W)
    each = pltpu.VMEM((TOP, PARTICLES, LANES), f32)
    sums = call(
        gather_kernel,
        "gather",
        shape((OWNERS, 8, SEND_W), bf16),
        [SM] + [VM] * 4,
        (idx, post, table, wre, wim),
        [each, each, rows, rows],
    )
    arrived = lax.all_to_all(sums, CLS, 0, 0, tiled=True)
    return call(
        final_kernel, "final", shape((7, 2 * IMG_W), f32), [VM, VM], (arrived, spread)
    )


def solution(mesh):
    finer = Mesh(mesh.devices.reshape(2, 2, 8, 8), DEVICES)
    in_specs = (
        P(DEVICES, None),
        P(DEVICES, None),
        P(DEVICES, None),
        P(),
        P(CLS, None),
        P(),
    )
    return jax.shard_map(
        on_device, mesh=finer, in_specs=in_specs, out_specs=P(CLS, "img"), check_vma=False
    )
```

time: 103 us -> 98.1 us (0.952)
  blocking collectives: 59.6 us -> 43.8 us
  waiting for transfers between devices: 10 us -> 19.6 us
  local copies, waits for them, and re-layouts: 7.96 us -> 1.44 us
  starting transfers between devices: 10.9 us -> 16.6 us
  Pallas kernels: 13.8 us -> 15.7 us
    all_to_all x1 -> x0, blocking collectives: 15.4 us -> none  [on_device(): lax.all_to_all(wsend, GROUP, 0, 0, tiled=True).reshape(PARTICLES, SEND_W)]
    all_to_all x0 -> x1, waiting for transfers between devices: none -> 9.31 us  [on_device(): wrecv = lax.all_to_all(wsend, GROUP, 0, 0, tiled=True)]
    unnamed x25 -> x12, local copies, waits for them, and re-layouts: 7.53 us -> 1.04 us
    all_to_all x0 -> x1, starting transfers between devices: none -> 5.63 us  [on_device(): wrecv = lax.all_to_all(wsend, GROUP, 0, 0, tiled=True)]
    pallas_call x6 -> x7, Pallas kernels: 13.8 us -> 15.7 us  [call(): pl.pallas_call(kernel, out_shape=out_shape, in_specs=in_specs, out_specs=...]
  transfers between devices with their start and end apart: 1 -> 2, of which waited for: 1 -> 2; matrix products, arithmetic and copies ran while one was open for 1% -> 1% of each run, Pallas kernels for 1% -> 2%
where the time goes in v3:
time: 98.1 us; the launch traced here: 97.6 us
  blocking collectives  43.8 us (45%)
  waiting for transfers between devices  19.6 us (20%)
  starting transfers between devices  16.6 us (17%)
  Pallas kernels  15.7 us (16%)
  local copies, waits for them, and re-layouts  1.44 us (1%)
    all_to_all x1, blocking collectives, on_device(): arrived = lax.all_to_all(sums, CLS, 0, 0, tiled=True)  21.2 us
    pallas_call x7, Pallas kernels, call(): pl.pallas_call(kernel, out_shape=out_shape, in_specs=in_specs, out_specs=...  15.7 us
    all_to_all x1, blocking collectives, on_device(): lax.all_to_all(partial.reshape(MEMBERS, 16, LOGIT_W), GROUP, 0, 0, tiled=...  12.6 us
    all_to_all x1, starting transfers between devices, on_device(): rrecv = lax.all_to_all(rsend, CLS, 0, 0, tiled=True)  10.9 us
    all_to_all x1, waiting for transfers between devices, on_device(): rrecv = lax.all_to_all(rsend, CLS, 0, 0, tiled=True)  10.3 us
    all_to_all x1, blocking collectives, on_device(): lax.all_to_all(post, GROUP, 0, 0, tiled=True).reshape(PARTICLES, LOGIT_W)  9.97 us
    all_to_all x1, waiting for transfers between devices, on_device(): wrecv = lax.all_to_all(wsend, GROUP, 0, 0, tiled=True)  9.31 us
    all_to_all x1, starting transfers between devices, on_device(): wrecv = lax.all_to_all(wsend, GROUP, 0, 0, tiled=True)  5.63 us
  transfers between devices with their start and end apart: 2, of which 2 were waited for; matrix products, arithmetic and copies ran while one was open for 1% of the time, Pallas kernels for 2%

profile of v3, /device:TPU:32, one launch (start us, length us, event | category | flops | bytes accessed | tf_op | source)
XLA Modules:
  0.0 97.6 jit_solution(2066560869426891230)
XLA Ops:
  0.0 2.1 %pack.1 = bf16[16,16,896]{2,1,0:T(8,128)(2,1)} custom-call(bf16[16,9216]{1,0:T(8,128)(2,1)} %images.1, bf16[16,4608]{1,0:T(8,128)(2,1)} %ctf.1, s32[4,16]{1,0:T(4,128)} %bitcast.9, s32[1,224]{1,0:T(1,128)} %bitcast.10), custom_call_target="tpu_custom_call" | custom-call | tf_op jit(solution)/shard_map/pack/pallas_call | solution.py:318
  2.1 0.0 copy-start.4
  2.1 5.6 %all-to-all-start = ((bf16[16,16,896]{2,1,0:T(8,128)(2,1)}), bf16[16,16,896]{2,1,0:T(8,128)(2,1)S(1)}, u32[]{:S(2)}, u32[]{:S(2)}) async-start(bf16[16,16,896]{2,1,0:T(8,128)(2,1)} %pack.1), calls=%async_computation | async-start | bytes 917504 | tf_op jit(solution)/shard_map/all_to_all | solution.py:349
  7.7 0.0 copy-start.1
  7.7 0.0 copy-done.4
  7.7 0.0 copy-start
  7.8 0.8 copies.1
  8.6 9.3 %all-to-all-done = bf16[16,16,896]{2,1,0:T(8,128)(2,1)S(1)} async-done(((bf16[16,16,896]{2,1,0:T(8,128)(2,1)}), bf16[16,16,896]{2,1,0:T(8,128)(2,1)S(1)}, u32[]{:S(2)}, u32[]{:S(2)}) %all-to-all-start) | async-done | bytes 458784 | tf_op jit(solution)/shard_map/all_to_all | solution.py:349
  17.9 10.9 %all-to-all-start.1 = ((bf16[32,8,640]{2,1,0:T(8,128)(2,1)}), bf16[32,8,640]{2,1,0:T(8,128)(2,1)}, u32[]{:S(2)}, u32[]{:S(2)}) async-start(bf16[32,8,640]{2,1,0:T(8,128)(2,1)} %copies.1), calls=%async_computation.1 | async-start | bytes 655360 | tf_op jit(solution)/shard_map/all_to_all | solution.py:350
  28.8 0.0 copy-done.5
  28.8 0.1 dynamic-slice_divide_fusion
  28.9 0.1 broadcast_in_dim.10
  29.0 0.1 reshape.32
  29.1 0.1 broadcast_in_dim.9
  29.1 0.1 reshape.31
  29.2 0.1 pad_maximum_fusion
  29.3 0.2 fusion.3
  29.5 0.1 reshape.28.idx
  29.6 0.0 copy-done.2
  29.6 0.0 copy-done.1
  29.6 0.0 copy-done
  29.6 0.0 copy-start.3
  29.6 1.0 %copy-done.3 = bf16[16,16,896]{2,1,0:T(8,128)(2,1)S(1)} copy-done((bf16[16,16,896]{2,1,0:T(8,128)(2,1)S(1)}, bf16[16,16,896]{2,1,0:T(8,128)(2,1)}, u32[]{:S(2)}) %copy-start.3) | copy-done | bytes 458776
  30.6 1.1 %weigh.1 = (f32[2048,128]{1,0:T(8,128)S(1)}, f32[2048,128]{1,0:T(8,128)S(1)}) custom-call(bf16[256,896]{1,0:T(8,128)(2,1)S(1)} %bitcast.6, f32[1,896]{1,0:T(1,128)S(1)} %reshape.33.inv, bf16[384,896]{1,0:T(8,128)(2,1)S(1)} %copy-done.1, bf16[3,384,256]{2,1,0:T(8,128)(2,1)S(1)} %copy-done), custom_call_target="tpu_custom_call" | custom-call | tf_op jit(solution)/shard_map/weigh/pallas_call | solution.py:318
  31.7 10.3 %all-to-all-done.1.recv = bf16[32,8,640]{2,1,0:T(8,128)(2,1)} async-done(((bf16[32,8,640]{2,1,0:T(8,128)(2,1)}), bf16[32,8,640]{2,1,0:T(8,128)(2,1)}, u32[]{:S(2)}, u32[]{:S(2)}) %all-to-all-start.1) | async-done | bytes 327712 | tf_op jit(solution)/shard_map/all_to_all | solution.py:350
  42.0 5.3 %score.1 = f32[256,384]{1,0:T(8,128)S(1)} custom-call(s32[1024]{0:T(1024)S(1)} %reshape.28.idx, bf16[32,8,640]{2,1,0:T(8,128)(2,1)} %all-to-all-done.1.recv, bf16[3,384,256]{2,1,0:T(8,128)(2,1)S(1)} %copy-done, f32[2048,128]{1,0:T(8,128)S(1)} %get-tuple-element.7.wre, f32[2048,128]{1,0:T(8,128)S(1)} %get-tuple-element.8.wim), custom_call_target="tpu_custom_call" | custom-call | tf_op jit(solution)/shard_map/score/pallas_call | solution.py:318
  47.3 12.6 %all_to_all.25.parts = f32[16,16,384]{2,1,0:T(8,128)S(1)} all-to-all(f32[16,16,384]{2,1,0:T(8,128)S(1)} %bitcast.7), channel_id=1, replica_groups=mesh['xh'=2,'xl'=2,'z'=8,'img'=8] {'xl','img'}, dimensions={0} | all-to-all | bytes 786432 | tf_op jit(solution)/shard_map/all_to_all | solution.py:371
  59.9 0.2 softmax.1
  60.1 10.0 %all_to_all.26 = bf16[16,16,384]{2,1,0:T(8,128)(2,1)S(1)} all-to-all(bf16[16,16,384]{2,1,0:T(8,128)(2,1)S(1)} %softmax.1), channel_id=1, replica_groups=mesh['xh'=2,'xl'=2,'z'=8,'img'=8] {'xl','img'}, dimensions={0} | all-to-all | bytes 393216 | tf_op jit(solution)/shard_map/all_to_all | solution.py:375
  70.1 5.0 %gather.1 = bf16[32,8,896]{2,1,0:T(8,128)(2,1)S(1)} custom-call(s32[1024]{0:T(1024)S(1)} %reshape.28.idx, bf16[256,384]{1,0:T(8,128)(2,1)S(1)} %bitcast.8, bf16[3,384,256]{2,1,0:T(8,128)(2,1)S(1)} %copy-done, f32[2048,128]{1,0:T(8,128)S(1)} %get-tuple-element.7.wre, f32[2048,128]{1,0:T(8,128)S(1)} %get-tuple-element.8.wim), custom_call_target="tpu_custom_call" | custom-call | tf_op jit(solution)/shard_map/gather/pallas_call | solution.py:318
  75.1 21.2 %all_to_all.27.parts = bf16[32,8,896]{2,1,0:T(8,128)(2,1)S(1)} all-to-all(bf16[32,8,896]{2,1,0:T(8,128)(2,1)S(1)} %gather.1), channel_id=1, replica_groups=mesh['xh'=2,'xl'=2,'z'=8,'img'=8] {'xh','xl','z'}, dimensions={0} | all-to-all | bytes 917504 | tf_op jit(solution)/shard_map/all_to_all | solution.py:385
  96.3 1.3 %final.1 = f32[7,1152]{1,0:T(8,128)} custom-call(bf16[32,8,896]{2,1,0:T(8,128)(2,1)S(1)} %all_to_all.27.parts, bf16[384,896]{1,0:T(8,128)(2,1)S(1)} %copy-done.1), custom_call_target="tpu_custom_call" | custom-call | tf_op jit(solution)/shard_map/final/pallas_call | solution.py:318
  (4 shorter events, 0.0 us)
Async XLA Ops:
  2.1 5.7 %copy-start.4 = (bf16[7,9216]{1,0:T(8,128)(2,1)S(1)}, bf16[7,9216]{1,0:T(8,128)(2,1)}, u32[]{:S(2)}) copy-start(bf16[7,9216]{1,0:T(8,128)(2,1)} %refs.1) | copy-start | bytes 387076
  2.1 26.8 %copy-start.5 = (f32[64]{0:T(128)S(1)}, f32[64]{0:T(128)}, u32[]{:S(2)}) copy-start(f32[64]{0:T(128)} %param.13) | copy-start | bytes 772
  2.1 15.8 %all-to-all-start = ((bf16[16,16,896]{2,1,0:T(8,128)(2,1)}), bf16[16,16,896]{2,1,0:T(8,128)(2,1)S(1)}, u32[]{:S(2)}, u32[]{:S(2)}) async-start(bf16[16,16,896]{2,1,0:T(8,128)(2,1)} %pack.1), calls=%async_computation | async-start | bytes 917504 | tf_op jit(solution)/shard_map/all_to_all | solution.py:349
  7.7 21.9 %copy-start.1 = (bf16[384,896]{1,0:T(8,128)(2,1)S(1)}, bf16[384,896]{1,0:T(8,128)(2,1)}, u32[]{:S(2)}) copy-start(bf16[384,896]{1,0:T(8,128)(2,1)} %constant.46.clone.spread) | copy-start | bytes 2064388
  7.7 21.8 %copy-start = (bf16[3,384,256]{2,1,0:T(8,128)(2,1)S(1)}, bf16[3,384,256]{2,1,0:T(8,128)(2,1)}, u32[]{:S(2)}) copy-start(bf16[3,384,256]{2,1,0:T(8,128)(2,1)} %constant.47.clone.table) | copy-start | bytes 1769476
  17.9 11.7 %copy-start.2 = (bf16[16,16,896]{2,1,0:T(8,128)(2,1)}, bf16[16,16,896]{2,1,0:T(8,128)(2,1)S(1)}, u32[]{:S(2)}) copy-start(bf16[16,16,896]{2,1,0:T(8,128)(2,1)S(1)} %all-to-all-done) | copy-start | bytes 1376260
  17.9 24.1 %all-to-all-start.1 = ((bf16[32,8,640]{2,1,0:T(8,128)(2,1)}), bf16[32,8,640]{2,1,0:T(8,128)(2,1)}, u32[]{:S(2)}, u32[]{:S(2)}) async-start(bf16[32,8,640]{2,1,0:T(8,128)(2,1)} %copies.1), calls=%async_computation.1 | async-start | bytes 655360 | tf_op jit(solution)/shard_map/all_to_all | solution.py:350
  29.6 1.0 %copy-start.3 = (bf16[16,16,896]{2,1,0:T(8,128)(2,1)S(1)}, bf16[16,16,896]{2,1,0:T(8,128)(2,1)}, u32[]{:S(2)}) copy-start(bf16[16,16,896]{2,1,0:T(8,128)(2,1)} %copy-done.2) | copy-start | bytes 1376260

commit v4 on v3

--- a/solution.py
+++ b/solution.py
@@ -11,7 +11,7 @@
 NA = 72
 HALF = 64
 LANES = 128
-PITCH = 8
+PITCH = 16
 SHELLS = 4
 WINDOWS = 6
 MEMBERS = 16
@@ -28,9 +28,9 @@
 FREQS = NA // 2 + 1
 TOPPAD = 112
 TABLE = 384
-CLS = ("xh", "xl", "z")
-GROUP = ("xl", "img")
-DEVICES = ("xh", "xl", "z", "img")
+CLS = ("x", "zh", "zl")
+GROUP = ("zl", "img")
+DEVICES = ("x", "zh", "zl", "img")
 
 bf16 = jnp.bfloat16
 f32 = jnp.float32
@@ -97,6 +97,18 @@
     freq = lane_index((1, LANES)) % HALF
     ends = (freq == 0) | (freq == NA // 2)
     return jnp.where(freq < FREQS, jnp.where(ends, 1.0 / NA, 2.0 / NA), 0.0).astype(f32)
+
+
+def put(hat, count, s, y):
+    hat[pl.ds(s, count, stride=PITCH), :] = y[:, :LANES]
+    hat[pl.ds(8 + s, count, stride=PITCH), :] = y[:, LANES:]
+
+
+def clear_rest(hat, count):
+    zero = jnp.zeros((count, LANES), f32)
+    for s in range(WINDOWS, 8):
+        hat[pl.ds(s, count, stride=PITCH), :] = zero
+        hat[pl.ds(8 + s, count, stride=PITCH), :] = zero
 
 
 def rows_summed(tiles):
@@ -145,24 +157,20 @@
         half = jnp.concatenate([half, jnp.zeros((7, REF_W - IMG_W), f32)], axis=1)
         half = jnp.concatenate([half, jnp.zeros((1, REF_W), f32)], axis=0).astype(bf16)
         for o in range(OWNERS):
-            if (o // 8) % 2 == h:
+            if o % 2 == h:
                 rsend[o] = half
 
 
-def weigh_kernel(recv, inv, spread, table, wre, wim):
+def weigh_kernel(recv, inv, spread, table, hat):
     scale = dot(recv[:, 512:], spread[...]) * inv[...]
     weighted = (recv[...].astype(f32) * scale).astype(bf16)
     for s in range(WINDOWS):
         y = forward_wave(lanes_of(weighted, s), table, s)
-        wre[pl.ds(s, PARTICLES, stride=PITCH), :] = y[:, :LANES]
-        wim[pl.ds(s, PARTICLES, stride=PITCH), :] = y[:, LANES:]
-    zero = jnp.zeros((PARTICLES, LANES), f32)
-    for s in range(WINDOWS, PITCH):
-        wre[pl.ds(s, PARTICLES, stride=PITCH), :] = zero
-        wim[pl.ds(s, PARTICLES, stride=PITCH), :] = zero
-
-
-def score_kernel(idx, recv, table, wre, wim, out, rre, rim, pq):
+        put(hat, PARTICLES, s, y)
+    clear_rest(hat, PARTICLES)
+
+
+def score_kernel(idx, recv, table, what, out, rhat, pq):
     raw32 = recv[...].astype(f32).reshape(TABLE_ROWS, REF_W)
     raw = raw32.astype(bf16)
     square = raw32 * raw32
@@ -176,29 +184,23 @@
     power = jnp.where(even, left, jnp.where(odd, right, 0.0)).astype(bf16).astype(f32)
     power = (-0.5 * power).astype(bf16)
     for s in range(SHELLS):
-        y = forward_wave(lanes_of(raw, s), table, s)
-        rre[pl.ds(s, TABLE_ROWS, stride=PITCH), :] = y[:, :LANES]
-        rim[pl.ds(s, TABLE_ROWS, stride=PITCH), :] = y[:, LANES:]
+        put(rhat, TABLE_ROWS, s, forward_wave(lanes_of(raw, s), table, s))
     for j in range(SHELLS // 2):
         y = sum(forward_wave(lanes_of(power, s), table, s) for s in (2 * j, 2 * j + 1))
-        rre[pl.ds(SHELLS + j, TABLE_ROWS, stride=PITCH), :] = y[:, :LANES]
-        rim[pl.ds(SHELLS + j, TABLE_ROWS, stride=PITCH), :] = y[:, LANES:]
-    zero = jnp.zeros((TABLE_ROWS, LANES), f32)
-    for s in range(WINDOWS, PITCH):
-        rre[pl.ds(s, TABLE_ROWS, stride=PITCH), :] = zero
-        rim[pl.ds(s, TABLE_ROWS, stride=PITCH), :] = zero
+        put(rhat, TABLE_ROWS, SHELLS + j, y)
+    clear_rest(rhat, TABLE_ROWS)
 
     def block(b, carry):
         rows = [[[], []] for _ in range(TOP)]
+        first = b // 2 * 64 + b % 2 * 8
         for u in range(8):
-            i = b * 8 + u
-            at = pl.multiple_of(i * PITCH, PITCH)
-            a_re = wre[pl.ds(at, PITCH), :]
-            a_im = wim[pl.ds(at, PITCH), :]
+            at = pl.multiple_of((b * 8 + u) * PITCH, PITCH)
+            a_re = what[pl.ds(at, 8), :]
+            a_im = what[pl.ds(at + 8, 8), :]
             for j in range(TOP):
-                t = pl.multiple_of(idx[b // 2 * 64 + j * 16 + b % 2 * 8 + u] * PITCH, PITCH)
-                b_re = rre[pl.ds(t, PITCH), :]
-                b_im = rim[pl.ds(t, PITCH), :]
+                t = pl.multiple_of(idx[first + (j * 16 + u)], PITCH)
+                b_re = rhat[pl.ds(t, 8), :]
+                b_im = rhat[pl.ds(t + 8, 8), :]
                 p = a_re * b_re + a_im * b_im
                 q = a_im * b_re - a_re * b_im
                 rows[j][0].append(p)
@@ -209,7 +211,7 @@
             pq[j, pl.ds(at, 8), LANES:] = rows_summed(rows[j][1])
         return carry
 
-    lax.fori_loop(0, PARTICLES // 8, block, 0)
+    lax.fori_loop(0, PARTICLES // 8, block, 0, unroll=4)
     weights = inverse_weights()
     low = lane_index((1, LANES)) < HALF
     windows = []
@@ -246,43 +248,45 @@
         out[k] = posterior
 
 
-def gather_kernel(idx, post, table, wre, wim, out, gre, gim, are, aim):
+def gather_kernel(idx, post, table, what, out, waves, total):
     lane = lane_index((1, 2 * LANES))
     for j in range(TOP):
         first = 16 * (j // 2) + NA * (j % 2)
         mine = (lane >= first) & (lane < first + NA)
         x = jnp.where(mine, lanes_of(post[...].astype(f32), j // 2), 0.0).astype(bf16)
         y = forward_wave(x, table, j // 2, splits=2)
-        gre[j] = y[:, :LANES] + pltpu.roll(y[:, :LANES], HALF, 1)
-        gim[j] = y[:, LANES:] + pltpu.roll(y[:, LANES:], HALF, 1)
-    are[...] = jnp.zeros_like(are)
-    aim[...] = jnp.zeros_like(aim)
+        waves[2 * j] = y[:, :LANES] + pltpu.roll(y[:, :LANES], HALF, 1)
+        waves[2 * j + 1] = y[:, LANES:] + pltpu.roll(y[:, LANES:], HALF, 1)
+    total[...] = jnp.zeros_like(total)
 
     def block(b, carry):
-        for u in range(4):
-            i = b * 4 + u
-            at = pl.multiple_of(i * PITCH, PITCH)
-            a_re = wre[pl.ds(at, PITCH), :]
-            a_im = wim[pl.ds(at, PITCH), :]
+        first = b // 2 * 64 + b % 2 * 8
+        lines = pl.ds(pl.multiple_of(b * 8, 8), 8)
+        tiles = [waves[k, lines, :] for k in range(2 * TOP)]
+        for u in range(8):
+            at = pl.multiple_of((b * 8 + u) * PITCH, PITCH)
+            a_re = what[pl.ds(at, 8), :]
+            a_im = what[pl.ds(at + 8, 8), :]
             pending = []
             for j in range(TOP):
-                where = b // 4 * 64 + j * 16 + b % 4 * 4 + u
-                t = pl.multiple_of(idx[where] * PITCH, PITCH)
-                g_re = gre[j, pl.ds(i, 1), :]
-                g_im = gim[j, pl.ds(i, 1), :]
-                pending.append((are, t, are[pl.ds(t, PITCH), :] + (a_re * g_re + a_im * g_im)))
-                pending.append((aim, t, aim[pl.ds(t, PITCH), :] + (a_im * g_re - a_re * g_im)))
-            for ref, t, value in pending:
-                ref[pl.ds(t, PITCH), :] = value
+                t = pl.multiple_of(idx[first + (j * 16 + u)], PITCH)
+                g_re = tiles[2 * j][u : u + 1]
+                g_im = tiles[2 * j + 1][u : u + 1]
+                re = total[pl.ds(t, 8), :] + (a_re * g_re + a_im * g_im)
+                im = total[pl.ds(t + 8, 8), :] + (a_im * g_re - a_re * g_im)
+                pending.append((t, re, im))
+            for t, re, im in pending:
+                total[pl.ds(t, 8), :] = re
+                total[pl.ds(t + 8, 8), :] = im
         return carry
 
-    lax.fori_loop(0, PARTICLES // 4, block, 0)
+    lax.fori_loop(0, PARTICLES // 8, block, 0)
     weights = inverse_weights()
     before = None
     for s in range(WINDOWS):
-        lines = pl.ds(s, TABLE_ROWS, stride=PITCH)
         x = jnp.concatenate(
-            [are[lines, :] * weights, aim[lines, :] * weights], axis=1
+            [total[pl.ds(8 * k + s, TABLE_ROWS, stride=PITCH), :] * weights for k in range(2)],
+            axis=1,
         )
         hi = x.astype(bf16)
         low = (x - hi.astype(f32)).astype(bf16)
@@ -297,7 +301,7 @@
 def final_kernel(parts, spread, out):
     sums = []
     for h in range(2):
-        members = [s for s in range(OWNERS) if (s // 8) % 2 == h]
+        members = [s for s in range(OWNERS) if s % 2 == h]
         total = parts[members[0]].astype(f32)
         for s in members[1:]:
             total += parts[s].astype(f32)
@@ -328,7 +332,7 @@
 
 def on_device(images, ctf, classes, class_place, references, sigma2):
     table, spread = make_tables()
-    img, h = lax.axis_index("img"), lax.axis_index("xl")
+    img, h = lax.axis_index("img"), lax.axis_index("zl")
     shape = jax.ShapeDtypeStruct
     wsend = call(
         pack_kernel,
@@ -349,38 +353,38 @@
     wrecv = lax.all_to_all(wsend, GROUP, 0, 0, tiled=True)
     rrecv = lax.all_to_all(rsend, CLS, 0, 0, tiled=True)
     listed = wrecv[:, :TOP, ROW_W : ROW_W + 16].astype(jnp.int32)
-    idx = (listed // 7 * 8 + listed % 7).reshape(-1)
+    idx = ((listed // 7 * 8 + listed % 7) * PITCH).reshape(-1)
     wrecv = wrecv.reshape(PARTICLES, SEND_W)
     inv = 1.0 / lax.dynamic_slice(sigma2, (img * 8 + h * SHELLS,), (SHELLS,))
     inv = jnp.concatenate(
         [jnp.repeat(inv, PAIR), jnp.repeat(inv, NA), jnp.zeros((SEND_W - ROW_W,), f32)]
     ).reshape(1, SEND_W)
     hat = shape((PARTICLES * PITCH, LANES), f32)
-    wre, wim = call(
-        weigh_kernel, "weigh", (hat, hat), [VM] * 4, (wrecv, inv, spread, table)
+    what = call(
+        weigh_kernel, "weigh", hat, [VM] * 4, (wrecv, inv, spread, table)
     )
     rows = pltpu.VMEM((TABLE_ROWS * PITCH, LANES), f32)
     partial = call(
         score_kernel,
         "score",
         shape((PARTICLES, LOGIT_W), f32),
-        [SM] + [VM] * 4,
-        (idx, rrecv, table, wre, wim),
-        [rows, rows, pltpu.VMEM((TOP, PARTICLES, 2 * LANES), f32)],
+        [SM] + [VM] * 3,
+        (idx, rrecv, table, what),
+        [rows, pltpu.VMEM((TOP, PARTICLES, 2 * LANES), f32)],
     )
     parts = lax.all_to_all(partial.reshape(MEMBERS, 16, LOGIT_W), GROUP, 0, 0, tiled=True)
     post = call(
         softmax_kernel, "softmax", shape((MEMBERS, 16, LOGIT_W), bf16), [VM], (parts,)
     )
     post = lax.all_to_all(post, GROUP, 0, 0, tiled=True).reshape(PARTICLES, LOGIT_W)
-    each = pltpu.VMEM((TOP, PARTICLES, LANES), f32)
+    waves = pltpu.VMEM((2 * TOP, PARTICLES, LANES), f32)
     sums = call(
         gather_kernel,
         "gather",
         shape((OWNERS, 8, SEND_W), bf16),
-        [SM] + [VM] * 4,
-        (idx, post, table, wre, wim),
-        [each, each, rows, rows],
+        [SM] + [VM] * 3,
+        (idx, post, table, what),
+        [waves, rows],
     )
     arrived = lax.all_to_all(sums, CLS, 0, 0, tiled=True)
     return call(
@@ -389,7 +393,7 @@
 
 
 def solution(mesh):
-    finer = Mesh(mesh.devices.reshape(2, 2, 8, 8), DEVICES)
+    finer = Mesh(mesh.devices.reshape(4, 4, 2, 8), DEVICES)
     in_specs = (
         P(DEVICES, None),
         P(DEVICES, None),

time: 98.1 us -> 96.5 us (0.984)
  waiting for transfers between devices: 19.6 us -> 17 us
  starting transfers between devices: 16.6 us -> 17.6 us
    all_to_all x1, waiting for transfers between devices: 9.31 us -> 7.07 us  [on_device(): wrecv = lax.all_to_all(wsend, GROUP, 0, 0, tiled=True)]
where the time goes in v4:
time: 96.5 us; the launch traced here: 96 us
  blocking collectives  43.5 us (45%)
  starting transfers between devices  17.6 us (18%)
  waiting for transfers between devices  17 us (18%)
  Pallas kernels  15.1 us (16%)
  local copies, waits for them, and re-layouts  2.34 us (2%)
    all_to_all x1, blocking collectives, on_device(): arrived = lax.all_to_all(sums, CLS, 0, 0, tiled=True)  20.8 us
    pallas_call x7, Pallas kernels, call(): pl.pallas_call(kernel, out_shape=out_shape, in_specs=in_specs, out_specs=...  15.1 us
    all_to_all x1, blocking collectives, on_device(): lax.all_to_all(partial.reshape(MEMBERS, 16, LOGIT_W), GROUP, 0, 0, tiled=...  12.6 us
    all_to_all x1, starting transfers between devices, on_device(): rrecv = lax.all_to_all(rsend, CLS, 0, 0, tiled=True)  11.7 us
    all_to_all x1, blocking collectives, on_device(): lax.all_to_all(post, GROUP, 0, 0, tiled=True).reshape(PARTICLES, LOGIT_W)  10.1 us
    all_to_all x1, waiting for transfers between devices, on_device(): rrecv = lax.all_to_all(rsend, CLS, 0, 0, tiled=True)  9.97 us
    all_to_all x1, waiting for transfers between devices, on_device(): wrecv = lax.all_to_all(wsend, GROUP, 0, 0, tiled=True)  7.07 us
    all_to_all x1, starting transfers between devices, on_device(): wrecv = lax.all_to_all(wsend, GROUP, 0, 0, tiled=True)  5.95 us
  transfers between devices with their start and end apart: 2, of which 2 were waited for; matrix products, arithmetic and copies ran while one was open for 1% of the time, Pallas kernels for 2%

profile of v4, /device:TPU:32, one launch (start us, length us, event | category | flops | bytes accessed | tf_op | source)
XLA Modules:
  0.0 96.0 jit_solution(13050556589248676914)
XLA Ops:
  0.0 0.0 copy-start
  0.0 0.0 copy-start.1
  0.0 0.0 copy-start.5
  0.0 2.2 %pack.1 = bf16[16,16,896]{2,1,0:T(8,128)(2,1)} custom-call(bf16[16,9216]{1,0:T(8,128)(2,1)} %images.1, bf16[16,4608]{1,0:T(8,128)(2,1)} %ctf.1, s32[4,16]{1,0:T(4,128)} %bitcast.9, s32[1,224]{1,0:T(1,128)} %bitcast.10), custom_call_target="tpu_custom_call" | custom-call | tf_op jit(solution)/shard_map/pack/pallas_call | solution.py:322
  2.2 5.9 %all-to-all-start = ((bf16[16,16,896]{2,1,0:T(8,128)(2,1)}), bf16[16,16,896]{2,1,0:T(8,128)(2,1)S(1)}, u32[]{:S(2)}, u32[]{:S(2)}) async-start(bf16[16,16,896]{2,1,0:T(8,128)(2,1)} %pack.1), calls=%async_computation | async-start | bytes 917504 | tf_op jit(solution)/shard_map/all_to_all | solution.py:353
  8.1 0.9 copy-done.4
  9.0 0.8 copies.1
  9.8 7.1 %all-to-all-done = bf16[16,16,896]{2,1,0:T(8,128)(2,1)S(1)} async-done(((bf16[16,16,896]{2,1,0:T(8,128)(2,1)}), bf16[16,16,896]{2,1,0:T(8,128)(2,1)S(1)}, u32[]{:S(2)}, u32[]{:S(2)}) %all-to-all-start) | async-done | bytes 458784 | tf_op jit(solution)/shard_map/all_to_all | solution.py:353
  16.9 11.7 %all-to-all-start.1 = ((bf16[32,8,640]{2,1,0:T(8,128)(2,1)}), bf16[32,8,640]{2,1,0:T(8,128)(2,1)}, u32[]{:S(2)}, u32[]{:S(2)}) async-start(bf16[32,8,640]{2,1,0:T(8,128)(2,1)} %copies.1), calls=%async_computation.1 | async-start | bytes 655360 | tf_op jit(solution)/shard_map/all_to_all | solution.py:354
  28.6 0.0 copy-done.5
  28.6 0.1 dynamic-slice_divide_fusion
  28.7 0.1 broadcast_in_dim.10
  28.8 0.1 reshape.32
  28.9 0.1 broadcast_in_dim.9
  28.9 0.1 reshape.31
  29.0 0.1 pad_maximum_fusion
  29.1 0.2 fusion.5
  29.3 0.1 reshape.28.idx
  29.4 0.0 copy-done.2
  29.4 0.0 copy-done
  29.4 0.0 copy-done.1
  29.4 0.0 copy-start.3
  29.4 1.0 %copy-done.3 = bf16[16,16,896]{2,1,0:T(8,128)(2,1)S(1)} copy-done((bf16[16,16,896]{2,1,0:T(8,128)(2,1)S(1)}, bf16[16,16,896]{2,1,0:T(8,128)(2,1)}, u32[]{:S(2)}) %copy-start.3) | copy-done | bytes 458776
  30.4 1.4 %weigh.1.what = f32[4096,128]{1,0:T(8,128)S(1)} custom-call(bf16[256,896]{1,0:T(8,128)(2,1)S(1)} %bitcast.6, f32[1,896]{1,0:T(1,128)S(1)} %reshape.33.inv, bf16[384,896]{1,0:T(8,128)(2,1)S(1)} %copy-done.1, bf16[3,384,256]{2,1,0:T(8,128)(2,1)S(1)} %copy-done), custom_call_target="tpu_custom_call" | custom-call | tf_op jit(solution)/shard_map/weigh/pallas_call | solution.py:322
  31.8 10.0 %all-to-all-done.1.recv = bf16[32,8,640]{2,1,0:T(8,128)(2,1)} async-done(((bf16[32,8,640]{2,1,0:T(8,128)(2,1)}), bf16[32,8,640]{2,1,0:T(8,128)(2,1)}, u32[]{:S(2)}, u32[]{:S(2)}) %all-to-all-start.1) | async-done | bytes 327712 | tf_op jit(solution)/shard_map/all_to_all | solution.py:354
  41.8 5.1 %score.1 = f32[256,384]{1,0:T(8,128)S(1)} custom-call(s32[1024]{0:T(1024)S(1)} %reshape.28.idx, bf16[32,8,640]{2,1,0:T(8,128)(2,1)} %all-to-all-done.1.recv, bf16[3,384,256]{2,1,0:T(8,128)(2,1)S(1)} %copy-done, f32[4096,128]{1,0:T(8,128)S(1)} %weigh.1.what), custom_call_target="tpu_custom_call" | custom-call | tf_op jit(solution)/shard_map/score/pallas_call | solution.py:322
  46.9 12.6 %all_to_all.25.parts = f32[16,16,384]{2,1,0:T(8,128)S(1)} all-to-all(f32[16,16,384]{2,1,0:T(8,128)S(1)} %bitcast.7), channel_id=1, replica_groups=mesh['x'=4,'zh'=4,'zl'=2,'img'=8] {'zl','img'}, dimensions={0} | all-to-all | bytes 786432 | tf_op jit(solution)/shard_map/all_to_all | solution.py:375
  59.5 0.2 softmax.1
  59.7 10.1 %all_to_all.26 = bf16[16,16,384]{2,1,0:T(8,128)(2,1)S(1)} all-to-all(bf16[16,16,384]{2,1,0:T(8,128)(2,1)S(1)} %softmax.1), channel_id=1, replica_groups=mesh['x'=4,'zh'=4,'zl'=2,'img'=8] {'zl','img'}, dimensions={0} | all-to-all | bytes 393216 | tf_op jit(solution)/shard_map/all_to_all | solution.py:379
  69.7 4.2 %gather.1 = bf16[32,8,896]{2,1,0:T(8,128)(2,1)S(1)} custom-call(s32[1024]{0:T(1024)S(1)} %reshape.28.idx, bf16[256,384]{1,0:T(8,128)(2,1)S(1)} %bitcast.8, bf16[3,384,256]{2,1,0:T(8,128)(2,1)S(1)} %copy-done, f32[4096,128]{1,0:T(8,128)S(1)} %weigh.1.what), custom_call_target="tpu_custom_call" | custom-call | tf_op jit(solution)/shard_map/gather/pallas_call | solution.py:322
  73.9 20.8 %all_to_all.27.parts = bf16[32,8,896]{2,1,0:T(8,128)(2,1)S(1)} all-to-all(bf16[32,8,896]{2,1,0:T(8,128)(2,1)S(1)} %gather.1), channel_id=1, replica_groups=mesh['x'=4,'zh'=4,'zl'=2,'img'=8] {'x','zh','zl'}, dimensions={0} | all-to-all | bytes 917504 | tf_op jit(solution)/shard_map/all_to_all | solution.py:389
  94.8 1.3 %final.1 = f32[7,1152]{1,0:T(8,128)} custom-call(bf16[32,8,896]{2,1,0:T(8,128)(2,1)S(1)} %all_to_all.27.parts, bf16[384,896]{1,0:T(8,128)(2,1)S(1)} %copy-done.1), custom_call_target="tpu_custom_call" | custom-call | tf_op jit(solution)/shard_map/final/pallas_call | solution.py:322
  (4 shorter events, 0.0 us)
Async XLA Ops:
  0.0 29.4 %copy-start = (bf16[3,384,256]{2,1,0:T(8,128)(2,1)S(1)}, bf16[3,384,256]{2,1,0:T(8,128)(2,1)}, u32[]{:S(2)}) copy-start(bf16[3,384,256]{2,1,0:T(8,128)(2,1)} %constant.48.clone.table) | copy-start | bytes 1769476
  0.0 29.4 %copy-start.1 = (bf16[384,896]{1,0:T(8,128)(2,1)S(1)}, bf16[384,896]{1,0:T(8,128)(2,1)}, u32[]{:S(2)}) copy-start(bf16[384,896]{1,0:T(8,128)(2,1)} %constant.47.clone.spread) | copy-start | bytes 2064388
  0.0 28.6 %copy-start.5 = (f32[64]{0:T(128)S(1)}, f32[64]{0:T(128)}, u32[]{:S(2)}) copy-start(f32[64]{0:T(128)} %param.13) | copy-start | bytes 772
  2.2 14.7 %all-to-all-start = ((bf16[16,16,896]{2,1,0:T(8,128)(2,1)}), bf16[16,16,896]{2,1,0:T(8,128)(2,1)S(1)}, u32[]{:S(2)}, u32[]{:S(2)}) async-start(bf16[16,16,896]{2,1,0:T(8,128)(2,1)} %pack.1), calls=%async_computation | async-start | bytes 917504 | tf_op jit(solution)/shard_map/all_to_all | solution.py:353
  8.1 0.9 copy-start.4
  16.9 12.5 %copy-start.2 = (bf16[16,16,896]{2,1,0:T(8,128)(2,1)}, bf16[16,16,896]{2,1,0:T(8,128)(2,1)S(1)}, u32[]{:S(2)}) copy-start(bf16[16,16,896]{2,1,0:T(8,128)(2,1)S(1)} %all-to-all-done) | copy-start | bytes 1376260
  16.9 24.8 %all-to-all-start.1 = ((bf16[32,8,640]{2,1,0:T(8,128)(2,1)}), bf16[32,8,640]{2,1,0:T(8,128)(2,1)}, u32[]{:S(2)}, u32[]{:S(2)}) async-start(bf16[32,8,640]{2,1,0:T(8,128)(2,1)} %copies.1), calls=%async_computation.1 | async-start | bytes 655360 | tf_op jit(solution)/shard_map/all_to_all | solution.py:354
  29.4 1.0 %copy-start.3 = (bf16[16,16,896]{2,1,0:T(8,128)(2,1)S(1)}, bf16[16,16,896]{2,1,0:T(8,128)(2,1)}, u32[]{:S(2)}) copy-start(bf16[16,16,896]{2,1,0:T(8,128)(2,1)} %copy-done.2) | copy-start | bytes 1376260

commit v5 on v4

--- a/solution.py
+++ b/solution.py
@@ -28,6 +28,7 @@
 FREQS = NA // 2 + 1
 TOPPAD = 112
 TABLE = 384
+UNROLL = 4
 CLS = ("x", "zh", "zl")
 GROUP = ("zl", "img")
 DEVICES = ("x", "zh", "zl", "img")
@@ -170,7 +171,9 @@
     clear_rest(hat, PARTICLES)
 
 
-def score_kernel(idx, recv, table, what, out, rhat, pq):
+def score_kernel(places, recv, table, what, out, rhat, pq, idx, sem):
+    copy = pltpu.make_async_copy(places, idx, sem)
+    copy.start()
     raw32 = recv[...].astype(f32).reshape(TABLE_ROWS, REF_W)
     raw = raw32.astype(bf16)
     square = raw32 * raw32
@@ -191,27 +194,26 @@
     clear_rest(rhat, TABLE_ROWS)
 
     def block(b, carry):
-        rows = [[[], []] for _ in range(TOP)]
         first = b // 2 * 64 + b % 2 * 8
+        lines = pl.ds(pl.multiple_of(b * 8, 8), 8)
+        rows = []
         for u in range(8):
             at = pl.multiple_of((b * 8 + u) * PITCH, PITCH)
-            a_re = what[pl.ds(at, 8), :]
-            a_im = what[pl.ds(at + 8, 8), :]
-            for j in range(TOP):
+            rows.append((what[pl.ds(at, 8), :], what[pl.ds(at + 8, 8), :]))
+        for j in range(TOP):
+            p, q = [], []
+            for u, (a_re, a_im) in enumerate(rows):
                 t = pl.multiple_of(idx[first + (j * 16 + u)], PITCH)
                 b_re = rhat[pl.ds(t, 8), :]
                 b_im = rhat[pl.ds(t + 8, 8), :]
-                p = a_re * b_re + a_im * b_im
-                q = a_im * b_re - a_re * b_im
-                rows[j][0].append(p)
-                rows[j][1].append(q)
-        at = pl.multiple_of(b * 8, 8)
-        for j in range(TOP):
-            pq[j, pl.ds(at, 8), :LANES] = rows_summed(rows[j][0])
-            pq[j, pl.ds(at, 8), LANES:] = rows_summed(rows[j][1])
+                p.append(a_re * b_re + a_im * b_im)
+                q.append(a_im * b_re - a_re * b_im)
+            pq[j, lines, :LANES] = rows_summed(p)
+            pq[j, lines, LANES:] = rows_summed(q)
         return carry
 
-    lax.fori_loop(0, PARTICLES // 8, block, 0, unroll=4)
+    copy.wait()
+    lax.fori_loop(0, PARTICLES // 8, block, 0, unroll=UNROLL)
     weights = inverse_weights()
     low = lane_index((1, LANES)) < HALF
     windows = []
@@ -248,7 +250,9 @@
         out[k] = posterior
 
 
-def gather_kernel(idx, post, table, what, out, waves, total):
+def gather_kernel(places, post, table, what, out, waves, total, idx, sem):
+    copy = pltpu.make_async_copy(places, idx, sem)
+    copy.start()
     lane = lane_index((1, 2 * LANES))
     for j in range(TOP):
         first = 16 * (j // 2) + NA * (j % 2)
@@ -280,6 +284,7 @@
                 total[pl.ds(t + 8, 8), :] = im
         return carry
 
+    copy.wait()
     lax.fori_loop(0, PARTICLES // 8, block, 0)
     weights = inverse_weights()
     before = None
@@ -315,6 +320,7 @@
 
 VM = pl.BlockSpec(memory_space=pltpu.VMEM)
 SM = pl.BlockSpec(memory_space=pltpu.SMEM)
+ANY = pl.BlockSpec(memory_space=pl.ANY)
 
 
 def call(kernel, name, out_shape, in_specs, args, scratch=(), limit=24):
@@ -364,13 +370,14 @@
         weigh_kernel, "weigh", hat, [VM] * 4, (wrecv, inv, spread, table)
     )
     rows = pltpu.VMEM((TABLE_ROWS * PITCH, LANES), f32)
+    places = [pltpu.SMEM((PARTICLES * TOP,), jnp.int32), pltpu.SemaphoreType.DMA]
     partial = call(
         score_kernel,
         "score",
         shape((PARTICLES, LOGIT_W), f32),
-        [SM] + [VM] * 3,
+        [ANY] + [VM] * 3,
         (idx, rrecv, table, what),
-        [rows, pltpu.VMEM((TOP, PARTICLES, 2 * LANES), f32)],
+        [rows, pltpu.VMEM((TOP, PARTICLES, 2 * LANES), f32), *places],
     )
     parts = lax.all_to_all(partial.reshape(MEMBERS, 16, LOGIT_W), GROUP, 0, 0, tiled=True)
     post = call(
@@ -382,9 +389,9 @@
         gather_kernel,
         "gather",
         shape((OWNERS, 8, SEND_W), bf16),
-        [SM] + [VM] * 3,
+        [ANY] + [VM] * 3,
         (idx, post, table, what),
-        [waves, rows],
+        [waves, rows, *places],
     )
     arrived = lax.all_to_all(sums, CLS, 0, 0, tiled=True)
     return call(

time: 96.5 us -> 96 us (level)
  no operation moved by 1% of the time
where the time goes in v5:
time: 96 us; the launch traced here: 95.5 us
  blocking collectives  43.5 us (45%)
  starting transfers between devices  17.6 us (18%)
  waiting for transfers between devices  17 us (18%)
  Pallas kernels  14.6 us (15%)
  local copies, waits for them, and re-layouts  2.34 us (2%)
    all_to_all x1, blocking collectives, on_device(): arrived = lax.all_to_all(sums, CLS, 0, 0, tiled=True)  20.8 us
    pallas_call x7, Pallas kernels, call(): pl.pallas_call(kernel, out_shape=out_shape, in_specs=in_specs, out_specs=...  14.6 us
    all_to_all x1, blocking collectives, on_device(): lax.all_to_all(partial.reshape(MEMBERS, 16, LOGIT_W), GROUP, 0, 0, tiled=...  12.6 us
    all_to_all x1, starting transfers between devices, on_device(): rrecv = lax.all_to_all(rsend, CLS, 0, 0, tiled=True)  11.7 us
    all_to_all x1, blocking collectives, on_device(): lax.all_to_all(post, GROUP, 0, 0, tiled=True).reshape(PARTICLES, LOGIT_W)  10.1 us
    all_to_all x1, waiting for transfers between devices, on_device(): rrecv = lax.all_to_all(rsend, CLS, 0, 0, tiled=True)  9.97 us
    all_to_all x1, waiting for transfers between devices, on_device(): wrecv = lax.all_to_all(wsend, GROUP, 0, 0, tiled=True)  7.07 us
    all_to_all x1, starting transfers between devices, on_device(): wrecv = lax.all_to_all(wsend, GROUP, 0, 0, tiled=True)  5.95 us
  transfers between devices with their start and end apart: 2, of which 2 were waited for; matrix products, arithmetic and copies ran while one was open for 1% of the time, Pallas kernels for 2%

profile of v5, /device:TPU:32, one launch (start us, length us, event | category | flops | bytes accessed | tf_op | source)
XLA Modules:
  0.0 95.5 jit_solution(6142666021094098545)
XLA Ops:
  0.0 0.0 copy-start
  0.0 0.0 copy-start.1
  0.0 0.0 copy-start.5
  0.0 2.2 %pack.1 = bf16[16,16,896]{2,1,0:T(8,128)(2,1)} custom-call(bf16[16,9216]{1,0:T(8,128)(2,1)} %images.1, bf16[16,4608]{1,0:T(8,128)(2,1)} %ctf.1, s32[4,16]{1,0:T(4,128)} %bitcast.9, s32[1,224]{1,0:T(1,128)} %bitcast.10), custom_call_target="tpu_custom_call" | custom-call | tf_op jit(solution)/shard_map/pack/pallas_call | solution.py:328
  2.2 5.9 %all-to-all-start = ((bf16[16,16,896]{2,1,0:T(8,128)(2,1)}), bf16[16,16,896]{2,1,0:T(8,128)(2,1)S(1)}, u32[]{:S(2)}, u32[]{:S(2)}) async-start(bf16[16,16,896]{2,1,0:T(8,128)(2,1)} %pack.1), calls=%async_computation | async-start | bytes 917504 | tf_op jit(solution)/shard_map/all_to_all | solution.py:359
  8.1 0.9 copy-done.4
  9.0 0.8 copies.1
  9.8 7.1 %all-to-all-done = bf16[16,16,896]{2,1,0:T(8,128)(2,1)S(1)} async-done(((bf16[16,16,896]{2,1,0:T(8,128)(2,1)}), bf16[16,16,896]{2,1,0:T(8,128)(2,1)S(1)}, u32[]{:S(2)}, u32[]{:S(2)}) %all-to-all-start) | async-done | bytes 458784 | tf_op jit(solution)/shard_map/all_to_all | solution.py:359
  16.9 11.7 %all-to-all-start.1 = ((bf16[32,8,640]{2,1,0:T(8,128)(2,1)}), bf16[32,8,640]{2,1,0:T(8,128)(2,1)}, u32[]{:S(2)}, u32[]{:S(2)}) async-start(bf16[32,8,640]{2,1,0:T(8,128)(2,1)} %copies.1), calls=%async_computation.1 | async-start | bytes 655360 | tf_op jit(solution)/shard_map/all_to_all | solution.py:360
  28.6 0.0 copy-done.5
  28.6 0.1 dynamic-slice_divide_fusion
  28.7 0.1 broadcast_in_dim.10
  28.8 0.1 reshape.32
  28.9 0.1 broadcast_in_dim.9
  28.9 0.1 reshape.31
  29.0 0.1 pad_maximum_fusion
  29.1 0.2 fusion.5
  29.3 0.1 reshape.28.places
  29.4 0.0 copy-done.2
  29.4 0.0 copy-done
  29.4 0.0 copy-done.1
  29.4 0.0 copy-start.3
  29.4 1.0 %copy-done.3 = bf16[16,16,896]{2,1,0:T(8,128)(2,1)S(1)} copy-done((bf16[16,16,896]{2,1,0:T(8,128)(2,1)S(1)}, bf16[16,16,896]{2,1,0:T(8,128)(2,1)}, u32[]{:S(2)}) %copy-start.3) | copy-done | bytes 458776
  30.4 1.4 %weigh.1.what = f32[4096,128]{1,0:T(8,128)S(1)} custom-call(bf16[256,896]{1,0:T(8,128)(2,1)S(1)} %bitcast.6, f32[1,896]{1,0:T(1,128)S(1)} %reshape.33.inv, bf16[384,896]{1,0:T(8,128)(2,1)S(1)} %copy-done.1, bf16[3,384,256]{2,1,0:T(8,128)(2,1)S(1)} %copy-done), custom_call_target="tpu_custom_call" | custom-call | tf_op jit(solution)/shard_map/weigh/pallas_call | solution.py:328
  31.8 10.0 %all-to-all-done.1.recv = bf16[32,8,640]{2,1,0:T(8,128)(2,1)} async-done(((bf16[32,8,640]{2,1,0:T(8,128)(2,1)}), bf16[32,8,640]{2,1,0:T(8,128)(2,1)}, u32[]{:S(2)}, u32[]{:S(2)}) %all-to-all-start.1) | async-done | bytes 327712 | tf_op jit(solution)/shard_map/all_to_all | solution.py:360
  41.8 5.2 %score.1 = f32[256,384]{1,0:T(8,128)S(1)} custom-call(s32[1024]{0:T(1024)S(1)} %reshape.28.places, bf16[32,8,640]{2,1,0:T(8,128)(2,1)} %all-to-all-done.1.recv, bf16[3,384,256]{2,1,0:T(8,128)(2,1)S(1)} %copy-done, f32[4096,128]{1,0:T(8,128)S(1)} %weigh.1.what), custom_call_target="tpu_custom_call" | custom-call | tf_op jit(solution)/shard_map/score/pallas_call | solution.py:328
  47.0 12.6 %all_to_all.25.parts = f32[16,16,384]{2,1,0:T(8,128)S(1)} all-to-all(f32[16,16,384]{2,1,0:T(8,128)S(1)} %bitcast.7), channel_id=1, replica_groups=mesh['x'=4,'zh'=4,'zl'=2,'img'=8] {'zl','img'}, dimensions={0} | all-to-all | bytes 786432 | tf_op jit(solution)/shard_map/all_to_all | solution.py:382
  59.5 0.2 softmax.1
  59.8 10.1 %all_to_all.26 = bf16[16,16,384]{2,1,0:T(8,128)(2,1)S(1)} all-to-all(bf16[16,16,384]{2,1,0:T(8,128)(2,1)S(1)} %softmax.1), channel_id=1, replica_groups=mesh['x'=4,'zh'=4,'zl'=2,'img'=8] {'zl','img'}, dimensions={0} | all-to-all | bytes 393216 | tf_op jit(solution)/shard_map/all_to_all | solution.py:386
  69.8 3.6 %gather.1 = bf16[32,8,896]{2,1,0:T(8,128)(2,1)S(1)} custom-call(s32[1024]{0:T(1024)S(1)} %reshape.28.places, bf16[256,384]{1,0:T(8,128)(2,1)S(1)} %bitcast.8, bf16[3,384,256]{2,1,0:T(8,128)(2,1)S(1)} %copy-done, f32[4096,128]{1,0:T(8,128)S(1)} %weigh.1.what), custom_call_target="tpu_custom_call" | custom-call | tf_op jit(solution)/shard_map/gather/pallas_call | solution.py:328
  73.5 20.8 %all_to_all.27.parts = bf16[32,8,896]{2,1,0:T(8,128)(2,1)S(1)} all-to-all(bf16[32,8,896]{2,1,0:T(8,128)(2,1)S(1)} %gather.1), channel_id=1, replica_groups=mesh['x'=4,'zh'=4,'zl'=2,'img'=8] {'x','zh','zl'}, dimensions={0} | all-to-all | bytes 917504 | tf_op jit(solution)/shard_map/all_to_all | solution.py:396
  94.3 1.3 %final.1 = f32[7,1152]{1,0:T(8,128)} custom-call(bf16[32,8,896]{2,1,0:T(8,128)(2,1)S(1)} %all_to_all.27.parts, bf16[384,896]{1,0:T(8,128)(2,1)S(1)} %copy-done.1), custom_call_target="tpu_custom_call" | custom-call | tf_op jit(solution)/shard_map/final/pallas_call | solution.py:328
  (4 shorter events, 0.0 us)
Async XLA Ops:
  0.0 29.4 %copy-start = (bf16[3,384,256]{2,1,0:T(8,128)(2,1)S(1)}, bf16[3,384,256]{2,1,0:T(8,128)(2,1)}, u32[]{:S(2)}) copy-start(bf16[3,384,256]{2,1,0:T(8,128)(2,1)} %constant.48.clone.table) | copy-start | bytes 1769476
  0.0 29.4 %copy-start.1 = (bf16[384,896]{1,0:T(8,128)(2,1)S(1)}, bf16[384,896]{1,0:T(8,128)(2,1)}, u32[]{:S(2)}) copy-start(bf16[384,896]{1,0:T(8,128)(2,1)} %constant.47.clone.spread) | copy-start | bytes 2064388
  0.0 28.6 %copy-start.5 = (f32[64]{0:T(128)S(1)}, f32[64]{0:T(128)}, u32[]{:S(2)}) copy-start(f32[64]{0:T(128)} %param.13) | copy-start | bytes 772
  2.2 14.7 %all-to-all-start = ((bf16[16,16,896]{2,1,0:T(8,128)(2,1)}), bf16[16,16,896]{2,1,0:T(8,128)(2,1)S(1)}, u32[]{:S(2)}, u32[]{:S(2)}) async-start(bf16[16,16,896]{2,1,0:T(8,128)(2,1)} %pack.1), calls=%async_computation | async-start | bytes 917504 | tf_op jit(solution)/shard_map/all_to_all | solution.py:359
  8.1 0.9 copy-start.4
  16.9 12.5 %copy-start.2 = (bf16[16,16,896]{2,1,0:T(8,128)(2,1)}, bf16[16,16,896]{2,1,0:T(8,128)(2,1)S(1)}, u32[]{:S(2)}) copy-start(bf16[16,16,896]{2,1,0:T(8,128)(2,1)S(1)} %all-to-all-done) | copy-start | bytes 1376260
  16.9 24.8 %all-to-all-start.1 = ((bf16[32,8,640]{2,1,0:T(8,128)(2,1)}), bf16[32,8,640]{2,1,0:T(8,128)(2,1)}, u32[]{:S(2)}, u32[]{:S(2)}) async-start(bf16[32,8,640]{2,1,0:T(8,128)(2,1)} %copies.1), calls=%async_computation.1 | async-start | bytes 655360 | tf_op jit(solution)/shard_map/all_to_all | solution.py:360
  29.4 1.0 %copy-start.3 = (bf16[16,16,896]{2,1,0:T(8,128)(2,1)S(1)}, bf16[16,16,896]{2,1,0:T(8,128)(2,1)}, u32[]{:S(2)}) copy-start(bf16[16,16,896]{2,1,0:T(8,128)(2,1)} %copy-done.2) | copy-start | bytes 1376260

commit v6 on v5

--- a/solution.py
+++ b/solution.py
@@ -163,7 +163,8 @@
 
 
 def weigh_kernel(recv, inv, spread, table, hat):
-    scale = dot(recv[:, 512:], spread[...]) * inv[...]
+    scale = dot(recv[:, 512:], spread[...]).reshape(PARTICLES // 8, 8, SEND_W) * inv[...][None]
+    scale = scale.reshape(PARTICLES, SEND_W)
     weighted = (recv[...].astype(f32) * scale).astype(bf16)
     for s in range(WINDOWS):
         y = forward_wave(lanes_of(weighted, s), table, s)
@@ -364,7 +365,8 @@
     inv = 1.0 / lax.dynamic_slice(sigma2, (img * 8 + h * SHELLS,), (SHELLS,))
     inv = jnp.concatenate(
         [jnp.repeat(inv, PAIR), jnp.repeat(inv, NA), jnp.zeros((SEND_W - ROW_W,), f32)]
-    ).reshape(1, SEND_W)
+    )
+    inv = jnp.broadcast_to(inv[None], (8, SEND_W))
     hat = shape((PARTICLES * PITCH, LANES), f32)
     what = call(
         weigh_kernel, "weigh", hat, [VM] * 4, (wrecv, inv, spread, table)

time: 96 us -> 96 us (level)
  no operation moved by 1% of the time
where the time goes in v6:
time: 96 us; the launch traced here: 95.5 us
  blocking collectives  43.5 us (45%)
  starting transfers between devices  17.6 us (18%)
  waiting for transfers between devices  17 us (18%)
  Pallas kernels  14.6 us (15%)
  local copies, waits for them, and re-layouts  2.33 us (2%)
    all_to_all x1, blocking collectives, on_device(): arrived = lax.all_to_all(sums, CLS, 0, 0, tiled=True)  20.8 us
    pallas_call x7, Pallas kernels, call(): pl.pallas_call(kernel, out_shape=out_shape, in_specs=in_specs, out_specs=...  14.6 us
    all_to_all x1, blocking collectives, on_device(): lax.all_to_all(partial.reshape(MEMBERS, 16, LOGIT_W), GROUP, 0, 0, tiled=...  12.6 us
    all_to_all x1, starting transfers between devices, on_device(): rrecv = lax.all_to_all(rsend, CLS, 0, 0, tiled=True)  11.7 us
    all_to_all x1, blocking collectives, on_device(): lax.all_to_all(post, GROUP, 0, 0, tiled=True).reshape(PARTICLES, LOGIT_W)  10.1 us
    all_to_all x1, waiting for transfers between devices, on_device(): rrecv = lax.all_to_all(rsend, CLS, 0, 0, tiled=True)  9.96 us
    all_to_all x1, waiting for transfers between devices, on_device(): wrecv = lax.all_to_all(wsend, GROUP, 0, 0, tiled=True)  7.07 us
    all_to_all x1, starting transfers between devices, on_device(): wrecv = lax.all_to_all(wsend, GROUP, 0, 0, tiled=True)  5.95 us
  transfers between devices with their start and end apart: 2, of which 2 were waited for; matrix products, arithmetic and copies ran while one was open for 1% of the time, Pallas kernels for 2%

profile of v6, /device:TPU:32, one launch (start us, length us, event | category | flops | bytes accessed | tf_op | source)
XLA Modules:
  0.0 95.5 jit_solution(4212512383674931373)
XLA Ops:
  0.0 0.0 copy-start.1
  0.0 0.0 copy-start
  0.0 0.0 copy-start.5
  0.0 2.2 %pack.1 = bf16[16,16,896]{2,1,0:T(8,128)(2,1)} custom-call(bf16[16,9216]{1,0:T(8,128)(2,1)} %images.1, bf16[16,4608]{1,0:T(8,128)(2,1)} %ctf.1, s32[4,16]{1,0:T(4,128)} %bitcast.9, s32[1,224]{1,0:T(1,128)} %bitcast.10), custom_call_target="tpu_custom_call" | custom-call | tf_op jit(solution)/shard_map/pack/pallas_call | solution.py:329
  2.2 5.9 %all-to-all-start = ((bf16[16,16,896]{2,1,0:T(8,128)(2,1)}), bf16[16,16,896]{2,1,0:T(8,128)(2,1)S(1)}, u32[]{:S(2)}, u32[]{:S(2)}) async-start(bf16[16,16,896]{2,1,0:T(8,128)(2,1)} %pack.1), calls=%async_computation | async-start | bytes 917504 | tf_op jit(solution)/shard_map/all_to_all | solution.py:360
  8.1 0.9 copy-done.4
  9.0 0.8 copies.1
  9.8 7.1 %all-to-all-done = bf16[16,16,896]{2,1,0:T(8,128)(2,1)S(1)} async-done(((bf16[16,16,896]{2,1,0:T(8,128)(2,1)}), bf16[16,16,896]{2,1,0:T(8,128)(2,1)S(1)}, u32[]{:S(2)}, u32[]{:S(2)}) %all-to-all-start) | async-done | bytes 458784 | tf_op jit(solution)/shard_map/all_to_all | solution.py:360
  16.9 11.7 %all-to-all-start.1 = ((bf16[32,8,640]{2,1,0:T(8,128)(2,1)}), bf16[32,8,640]{2,1,0:T(8,128)(2,1)}, u32[]{:S(2)}, u32[]{:S(2)}) async-start(bf16[32,8,640]{2,1,0:T(8,128)(2,1)} %copies.1), calls=%async_computation.1 | async-start | bytes 655360 | tf_op jit(solution)/shard_map/all_to_all | solution.py:361
  28.6 0.0 copy-done.5
  28.6 0.1 dynamic-slice_divide_fusion
  28.7 0.1 broadcast_in_dim.15
  28.8 0.1 reshape.29
  28.9 0.1 broadcast_in_dim.16
  28.9 0.1 reshape.30
  29.0 0.1 pad_maximum_fusion
  29.1 0.2 fusion.5
  29.3 0.1 reshape.26.places
  29.4 0.0 copy-done.2
  29.4 0.0 copy-done.1
  29.4 0.0 copy-done
  29.4 0.0 copy-start.3
  29.4 1.0 %copy-done.3 = bf16[16,16,896]{2,1,0:T(8,128)(2,1)S(1)} copy-done((bf16[16,16,896]{2,1,0:T(8,128)(2,1)S(1)}, bf16[16,16,896]{2,1,0:T(8,128)(2,1)}, u32[]{:S(2)}) %copy-start.3) | copy-done | bytes 458776
  30.4 1.4 %weigh.1.what = f32[4096,128]{1,0:T(8,128)S(1)} custom-call(bf16[256,896]{1,0:T(8,128)(2,1)S(1)} %bitcast.6, f32[8,896]{1,0:T(8,128)S(1)} %broadcast_in_dim.18.inv, bf16[384,896]{1,0:T(8,128)(2,1)S(1)} %copy-done.1, bf16[3,384,256]{2,1,0:T(8,128)(2,1)S(1)} %copy-done), custom_call_target="tpu_custom_call" | custom-call | tf_op jit(solution)/shard_map/weigh/pallas_call | solution.py:329
  31.8 10.0 %all-to-all-done.1.recv = bf16[32,8,640]{2,1,0:T(8,128)(2,1)} async-done(((bf16[32,8,640]{2,1,0:T(8,128)(2,1)}), bf16[32,8,640]{2,1,0:T(8,128)(2,1)}, u32[]{:S(2)}, u32[]{:S(2)}) %all-to-all-start.1) | async-done | bytes 327712 | tf_op jit(solution)/shard_map/all_to_all | solution.py:361
  41.8 5.2 %score.1 = f32[256,384]{1,0:T(8,128)S(1)} custom-call(s32[1024]{0:T(1024)S(1)} %reshape.26.places, bf16[32,8,640]{2,1,0:T(8,128)(2,1)} %all-to-all-done.1.recv, bf16[3,384,256]{2,1,0:T(8,128)(2,1)S(1)} %copy-done, f32[4096,128]{1,0:T(8,128)S(1)} %weigh.1.what), custom_call_target="tpu_custom_call" | custom-call | tf_op jit(solution)/shard_map/score/pallas_call | solution.py:329
  47.0 12.6 %all_to_all.25.parts = f32[16,16,384]{2,1,0:T(8,128)S(1)} all-to-all(f32[16,16,384]{2,1,0:T(8,128)S(1)} %bitcast.7), channel_id=1, replica_groups=mesh['x'=4,'zh'=4,'zl'=2,'img'=8] {'zl','img'}, dimensions={0} | all-to-all | bytes 786432 | tf_op jit(solution)/shard_map/all_to_all | solution.py:384
  59.5 0.2 softmax.1
  59.8 10.1 %all_to_all.26 = bf16[16,16,384]{2,1,0:T(8,128)(2,1)S(1)} all-to-all(bf16[16,16,384]{2,1,0:T(8,128)(2,1)S(1)} %softmax.1), channel_id=1, replica_groups=mesh['x'=4,'zh'=4,'zl'=2,'img'=8] {'zl','img'}, dimensions={0} | all-to-all | bytes 393216 | tf_op jit(solution)/shard_map/all_to_all | solution.py:388
  69.8 3.6 %gather.1 = bf16[32,8,896]{2,1,0:T(8,128)(2,1)S(1)} custom-call(s32[1024]{0:T(1024)S(1)} %reshape.26.places, bf16[256,384]{1,0:T(8,128)(2,1)S(1)} %bitcast.8, bf16[3,384,256]{2,1,0:T(8,128)(2,1)S(1)} %copy-done, f32[4096,128]{1,0:T(8,128)S(1)} %weigh.1.what), custom_call_target="tpu_custom_call" | custom-call | tf_op jit(solution)/shard_map/gather/pallas_call | solution.py:329
  73.5 20.8 %all_to_all.27.parts = bf16[32,8,896]{2,1,0:T(8,128)(2,1)S(1)} all-to-all(bf16[32,8,896]{2,1,0:T(8,128)(2,1)S(1)} %gather.1), channel_id=1, replica_groups=mesh['x'=4,'zh'=4,'zl'=2,'img'=8] {'x','zh','zl'}, dimensions={0} | all-to-all | bytes 917504 | tf_op jit(solution)/shard_map/all_to_all | solution.py:398
  94.3 1.3 %final.1 = f32[7,1152]{1,0:T(8,128)} custom-call(bf16[32,8,896]{2,1,0:T(8,128)(2,1)S(1)} %all_to_all.27.parts, bf16[384,896]{1,0:T(8,128)(2,1)S(1)} %copy-done.1), custom_call_target="tpu_custom_call" | custom-call | tf_op jit(solution)/shard_map/final/pallas_call | solution.py:329
  (4 shorter events, 0.0 us)
Async XLA Ops:
  0.0 29.4 %copy-start.1 = (bf16[384,896]{1,0:T(8,128)(2,1)S(1)}, bf16[384,896]{1,0:T(8,128)(2,1)}, u32[]{:S(2)}) copy-start(bf16[384,896]{1,0:T(8,128)(2,1)} %constant.47.clone.spread) | copy-start | bytes 2064388
  0.0 29.4 %copy-start = (bf16[3,384,256]{2,1,0:T(8,128)(2,1)S(1)}, bf16[3,384,256]{2,1,0:T(8,128)(2,1)}, u32[]{:S(2)}) copy-start(bf16[3,384,256]{2,1,0:T(8,128)(2,1)} %constant.48.clone.table) | copy-start | bytes 1769476
  0.0 28.6 %copy-start.5 = (f32[64]{0:T(128)S(1)}, f32[64]{0:T(128)}, u32[]{:S(2)}) copy-start(f32[64]{0:T(128)} %param.13) | copy-start | bytes 772
  2.2 14.7 %all-to-all-start = ((bf16[16,16,896]{2,1,0:T(8,128)(2,1)}), bf16[16,16,896]{2,1,0:T(8,128)(2,1)S(1)}, u32[]{:S(2)}, u32[]{:S(2)}) async-start(bf16[16,16,896]{2,1,0:T(8,128)(2,1)} %pack.1), calls=%async_computation | async-start | bytes 917504 | tf_op jit(solution)/shard_map/all_to_all | solution.py:360
  8.1 0.9 copy-start.4
  16.9 12.5 %copy-start.2 = (bf16[16,16,896]{2,1,0:T(8,128)(2,1)}, bf16[16,16,896]{2,1,0:T(8,128)(2,1)S(1)}, u32[]{:S(2)}) copy-start(bf16[16,16,896]{2,1,0:T(8,128)(2,1)S(1)} %all-to-all-done) | copy-start | bytes 1376260
  16.9 24.8 %all-to-all-start.1 = ((bf16[32,8,640]{2,1,0:T(8,128)(2,1)}), bf16[32,8,640]{2,1,0:T(8,128)(2,1)}, u32[]{:S(2)}, u32[]{:S(2)}) async-start(bf16[32,8,640]{2,1,0:T(8,128)(2,1)} %copies.1), calls=%async_computation.1 | async-start | bytes 655360 | tf_op jit(solution)/shard_map/all_to_all | solution.py:361
  29.4 1.0 %copy-start.3 = (bf16[16,16,896]{2,1,0:T(8,128)(2,1)S(1)}, bf16[16,16,896]{2,1,0:T(8,128)(2,1)}, u32[]{:S(2)}) copy-start(bf16[16,16,896]{2,1,0:T(8,128)(2,1)} %copy-done.2) | copy-start | bytes 1376260

commit v7 on v6

--- a/solution.py
+++ b/solution.py
@@ -28,7 +28,7 @@
 FREQS = NA // 2 + 1
 TOPPAD = 112
 TABLE = 384
-UNROLL = 4
+UNROLL = 2
 CLS = ("x", "zh", "zl")
 GROUP = ("zl", "img")
 DEVICES = ("x", "zh", "zl", "img")

time: 96 us -> 96.2 us (level)
  no operation moved by 1% of the time
where the time goes in v7:
time: 96.2 us; the launch traced here: 95.7 us
  blocking collectives  43.5 us (45%)
  starting transfers between devices  17.6 us (18%)
  waiting for transfers between devices  17 us (18%)
  Pallas kernels  14.8 us (15%)
  local copies, waits for them, and re-layouts  2.33 us (2%)
    all_to_all x1, blocking collectives, on_device(): arrived = lax.all_to_all(sums, CLS, 0, 0, tiled=True)  20.8 us
    pallas_call x7, Pallas kernels, call(): pl.pallas_call(kernel, out_shape=out_shape, in_specs=in_specs, out_specs=...  14.8 us
    all_to_all x1, blocking collectives, on_device(): lax.all_to_all(partial.reshape(MEMBERS, 16, LOGIT_W), GROUP, 0, 0, tiled=...  12.6 us
    all_to_all x1, starting transfers between devices, on_device(): rrecv = lax.all_to_all(rsend, CLS, 0, 0, tiled=True)  11.7 us
    all_to_all x1, blocking collectives, on_device(): lax.all_to_all(post, GROUP, 0, 0, tiled=True).reshape(PARTICLES, LOGIT_W)  10.1 us
    all_to_all x1, waiting for transfers between devices, on_device(): rrecv = lax.all_to_all(rsend, CLS, 0, 0, tiled=True)  9.96 us
    all_to_all x1, waiting for transfers between devices, on_device(): wrecv = lax.all_to_all(wsend, GROUP, 0, 0, tiled=True)  7.07 us
    all_to_all x1, starting transfers between devices, on_device(): wrecv = lax.all_to_all(wsend, GROUP, 0, 0, tiled=True)  5.95 us
  transfers between devices with their start and end apart: 2, of which 2 were waited for; matrix products, arithmetic and copies ran while one was open for 1% of the time, Pallas kernels for 2%

profile of v7, /device:TPU:32, one launch (start us, length us, event | category | flops | bytes accessed | tf_op | source)
XLA Modules:
  0.0 95.7 jit_solution(8396084931885712998)
XLA Ops:
  0.0 0.0 copy-start.1
  0.0 0.0 copy-start
  0.0 0.0 copy-start.5
  0.0 2.2 %pack.1 = bf16[16,16,896]{2,1,0:T(8,128)(2,1)} custom-call(bf16[16,9216]{1,0:T(8,128)(2,1)} %images.1, bf16[16,4608]{1,0:T(8,128)(2,1)} %ctf.1, s32[4,16]{1,0:T(4,128)} %bitcast.9, s32[1,224]{1,0:T(1,128)} %bitcast.10), custom_call_target="tpu_custom_call" | custom-call | tf_op jit(solution)/shard_map/pack/pallas_call | solution.py:329
  2.2 5.9 %all-to-all-start = ((bf16[16,16,896]{2,1,0:T(8,128)(2,1)}), bf16[16,16,896]{2,1,0:T(8,128)(2,1)S(1)}, u32[]{:S(2)}, u32[]{:S(2)}) async-start(bf16[16,16,896]{2,1,0:T(8,128)(2,1)} %pack.1), calls=%async_computation | async-start | bytes 917504 | tf_op jit(solution)/shard_map/all_to_all | solution.py:360
  8.1 0.9 copy-done.4
  9.0 0.8 copies.1
  9.8 7.1 %all-to-all-done = bf16[16,16,896]{2,1,0:T(8,128)(2,1)S(1)} async-done(((bf16[16,16,896]{2,1,0:T(8,128)(2,1)}), bf16[16,16,896]{2,1,0:T(8,128)(2,1)S(1)}, u32[]{:S(2)}, u32[]{:S(2)}) %all-to-all-start) | async-done | bytes 458784 | tf_op jit(solution)/shard_map/all_to_all | solution.py:360
  16.9 11.7 %all-to-all-start.1 = ((bf16[32,8,640]{2,1,0:T(8,128)(2,1)}), bf16[32,8,640]{2,1,0:T(8,128)(2,1)}, u32[]{:S(2)}, u32[]{:S(2)}) async-start(bf16[32,8,640]{2,1,0:T(8,128)(2,1)} %copies.1), calls=%async_computation.1 | async-start | bytes 655360 | tf_op jit(solution)/shard_map/all_to_all | solution.py:361
  28.6 0.0 copy-done.5
  28.6 0.1 dynamic-slice_divide_fusion
  28.7 0.1 broadcast_in_dim.15
  28.8 0.1 reshape.29
  28.9 0.1 broadcast_in_dim.16
  28.9 0.1 reshape.30
  29.0 0.1 pad_maximum_fusion
  29.1 0.2 fusion.5
  29.3 0.1 reshape.26.places
  29.4 0.0 copy-done.2
  29.4 0.0 copy-done.1
  29.4 0.0 copy-done
  29.4 0.0 copy-start.3
  29.4 1.0 %copy-done.3 = bf16[16,16,896]{2,1,0:T(8,128)(2,1)S(1)} copy-done((bf16[16,16,896]{2,1,0:T(8,128)(2,1)S(1)}, bf16[16,16,896]{2,1,0:T(8,128)(2,1)}, u32[]{:S(2)}) %copy-start.3) | copy-done | bytes 458776
  30.4 1.4 %weigh.1.what = f32[4096,128]{1,0:T(8,128)S(1)} custom-call(bf16[256,896]{1,0:T(8,128)(2,1)S(1)} %bitcast.6, f32[8,896]{1,0:T(8,128)S(1)} %broadcast_in_dim.18.inv, bf16[384,896]{1,0:T(8,128)(2,1)S(1)} %copy-done.1, bf16[3,384,256]{2,1,0:T(8,128)(2,1)S(1)} %copy-done), custom_call_target="tpu_custom_call" | custom-call | tf_op jit(solution)/shard_map/weigh/pallas_call | solution.py:329
  31.8 10.0 %all-to-all-done.1.recv = bf16[32,8,640]{2,1,0:T(8,128)(2,1)} async-done(((bf16[32,8,640]{2,1,0:T(8,128)(2,1)}), bf16[32,8,640]{2,1,0:T(8,128)(2,1)}, u32[]{:S(2)}, u32[]{:S(2)}) %all-to-all-start.1) | async-done | bytes 327712 | tf_op jit(solution)/shard_map/all_to_all | solution.py:361
  41.8 5.3 %score.1 = f32[256,384]{1,0:T(8,128)S(1)} custom-call(s32[1024]{0:T(1024)S(1)} %reshape.26.places, bf16[32,8,640]{2,1,0:T(8,128)(2,1)} %all-to-all-done.1.recv, bf16[3,384,256]{2,1,0:T(8,128)(2,1)S(1)} %copy-done, f32[4096,128]{1,0:T(8,128)S(1)} %weigh.1.what), custom_call_target="tpu_custom_call" | custom-call | tf_op jit(solution)/shard_map/score/pallas_call | solution.py:329
  47.1 12.6 %all_to_all.25.parts = f32[16,16,384]{2,1,0:T(8,128)S(1)} all-to-all(f32[16,16,384]{2,1,0:T(8,128)S(1)} %bitcast.7), channel_id=1, replica_groups=mesh['x'=4,'zh'=4,'zl'=2,'img'=8] {'zl','img'}, dimensions={0} | all-to-all | bytes 786432 | tf_op jit(solution)/shard_map/all_to_all | solution.py:384
  59.7 0.2 softmax.1
  59.9 10.1 %all_to_all.26 = bf16[16,16,384]{2,1,0:T(8,128)(2,1)S(1)} all-to-all(bf16[16,16,384]{2,1,0:T(8,128)(2,1)S(1)} %softmax.1), channel_id=1, replica_groups=mesh['x'=4,'zh'=4,'zl'=2,'img'=8] {'zl','img'}, dimensions={0} | all-to-all | bytes 393216 | tf_op jit(solution)/shard_map/all_to_all | solution.py:388
  69.9 3.6 %gather.1 = bf16[32,8,896]{2,1,0:T(8,128)(2,1)S(1)} custom-call(s32[1024]{0:T(1024)S(1)} %reshape.26.places, bf16[256,384]{1,0:T(8,128)(2,1)S(1)} %bitcast.8, bf16[3,384,256]{2,1,0:T(8,128)(2,1)S(1)} %copy-done, f32[4096,128]{1,0:T(8,128)S(1)} %weigh.1.what), custom_call_target="tpu_custom_call" | custom-call | tf_op jit(solution)/shard_map/gather/pallas_call | solution.py:329
  73.6 20.8 %all_to_all.27.parts = bf16[32,8,896]{2,1,0:T(8,128)(2,1)S(1)} all-to-all(bf16[32,8,896]{2,1,0:T(8,128)(2,1)S(1)} %gather.1), channel_id=1, replica_groups=mesh['x'=4,'zh'=4,'zl'=2,'img'=8] {'x','zh','zl'}, dimensions={0} | all-to-all | bytes 917504 | tf_op jit(solution)/shard_map/all_to_all | solution.py:398
  94.4 1.3 %final.1 = f32[7,1152]{1,0:T(8,128)} custom-call(bf16[32,8,896]{2,1,0:T(8,128)(2,1)S(1)} %all_to_all.27.parts, bf16[384,896]{1,0:T(8,128)(2,1)S(1)} %copy-done.1), custom_call_target="tpu_custom_call" | custom-call | tf_op jit(solution)/shard_map/final/pallas_call | solution.py:329
  (4 shorter events, 0.0 us)
Async XLA Ops:
  0.0 29.4 %copy-start.1 = (bf16[384,896]{1,0:T(8,128)(2,1)S(1)}, bf16[384,896]{1,0:T(8,128)(2,1)}, u32[]{:S(2)}) copy-start(bf16[384,896]{1,0:T(8,128)(2,1)} %constant.47.clone.spread) | copy-start | bytes 2064388
  0.0 29.4 %copy-start = (bf16[3,384,256]{2,1,0:T(8,128)(2,1)S(1)}, bf16[3,384,256]{2,1,0:T(8,128)(2,1)}, u32[]{:S(2)}) copy-start(bf16[3,384,256]{2,1,0:T(8,128)(2,1)} %constant.48.clone.table) | copy-start | bytes 1769476
  0.0 28.6 %copy-start.5 = (f32[64]{0:T(128)S(1)}, f32[64]{0:T(128)}, u32[]{:S(2)}) copy-start(f32[64]{0:T(128)} %param.13) | copy-start | bytes 772
  2.2 14.7 %all-to-all-start = ((bf16[16,16,896]{2,1,0:T(8,128)(2,1)}), bf16[16,16,896]{2,1,0:T(8,128)(2,1)S(1)}, u32[]{:S(2)}, u32[]{:S(2)}) async-start(bf16[16,16,896]{2,1,0:T(8,128)(2,1)} %pack.1), calls=%async_computation | async-start | bytes 917504 | tf_op jit(solution)/shard_map/all_to_all | solution.py:360
  8.1 0.9 copy-start.4
  16.9 12.5 %copy-start.2 = (bf16[16,16,896]{2,1,0:T(8,128)(2,1)}, bf16[16,16,896]{2,1,0:T(8,128)(2,1)S(1)}, u32[]{:S(2)}) copy-start(bf16[16,16,896]{2,1,0:T(8,128)(2,1)S(1)} %all-to-all-done) | copy-start | bytes 1376260
  16.9 24.8 %all-to-all-start.1 = ((bf16[32,8,640]{2,1,0:T(8,128)(2,1)}), bf16[32,8,640]{2,1,0:T(8,128)(2,1)}, u32[]{:S(2)}, u32[]{:S(2)}) async-start(bf16[32,8,640]{2,1,0:T(8,128)(2,1)} %copies.1), calls=%async_computation.1 | async-start | bytes 655360 | tf_op jit(solution)/shard_map/all_to_all | solution.py:361
  29.4 1.0 %copy-start.3 = (bf16[16,16,896]{2,1,0:T(8,128)(2,1)S(1)}, bf16[16,16,896]{2,1,0:T(8,128)(2,1)}, u32[]{:S(2)}) copy-start(bf16[16,16,896]{2,1,0:T(8,128)(2,1)} %copy-done.2) | copy-start | bytes 1376260
